TPU v7x, 256 devices: a whole 4x4x8 slice. The times are simulated.
256 devices in a mesh: ctx: 32 (over z, x), head: 8 (over y, core).
Axes of the slice: x: 4, y: 4, z: 8, core: 2. Of those that a mesh axis runs over, the one named last changes fastest.
Arguments:
- query_rows: bfloat16 [32768, 16, 128], P(('ctx', 'head')), may hold values from -6 to 6
- key_rows: bfloat16 [32768, 16, 128], P(('ctx', 'head')), may hold values from -4 to 4
- value_rows: bfloat16 [32768, 32, 128], P(('ctx', 'head')), may hold values from -6 to 6
- beta_rows: bfloat16 [32768, 32], P(('ctx', 'head')), may hold values from 0.0099 to 0.5
- log_gate: bfloat16 [32768, 32], P(('ctx', 'head')), may hold values from -0.75 to 0
Outputs:
- mixed_values: bfloat16 [32768, 32, 128], P(('ctx', 'head'))
All inputs are finite; a program needn't handle non-finite values.
Results may differ from a plain program's by a relative error of at most 0.0013.
Values may be sent and summed in bfloat16 or wider, within the bound.
No kernel may reach another device: no remote copies, remote signals or barrier semaphores. Data moves between devices by JAX's collectives and lax.ppermute only.
A program may use at most 128 MiB of HBM per device.

v0:
```python
import jax
import jax.numpy as jnp
from jax import lax
from jax.sharding import PartitionSpec as P

HK = 16
VALUE_HEADS = 32
DK = 128
DV = 128
BLK = 128


def entering(value, axis, join, neutral):
    count, mine = (lax.axis_size(axis), lax.axis_index(axis))
    pieces = jax.tree.map(lambda part: lax.all_gather(part, axis), value)
    subtotal = jax.tree.map(
        lambda part, zero: jnp.full_like(part, 0) + jnp.asarray(zero, part.dtype), value, neutral
    )

    def step(position, subtotal):
        longer = join(subtotal, jax.tree.map(lambda part: part[position], pieces))
        return jax.tree.map(lambda new, old: jnp.where(position < mine, new, old), longer, subtotal)

    return lax.fori_loop(0, count - 1, step, subtotal)


def unit_rows(source):
    widened = source.astype(jnp.float32)
    return widened * lax.rsqrt(jnp.sum(widened * widened, -1, keepdims=True) + 1e-06)


def sweep_blocks(initial, key_unit, queries, values, beta_vals, gate_logs, with_output):
    total_rows, head_count = gate_logs.shape
    block_count = total_rows // BLK
    row_total = initial.shape[1]
    split_at = row_total - DV
    token_places = jnp.arange(BLK)
    strict_lower = token_places[:, None] > token_places[None, :]
    inclusive = token_places[:, None] >= token_places[None, :]
    identity_block = jnp.eye(BLK, dtype=jnp.float32)
    highest = lax.Precision.HIGHEST

    def advance(carried, pieces):
        key_block, query_block, value_block, beta_block, gate_block = pieces
        cumulative = jnp.cumsum(gate_block, axis=0)
        cumul_heads = cumulative.T
        spread = jnp.minimum(cumul_heads[:, :, None] - cumul_heads[:, None, :], 0.0)
        decay_table = jnp.exp(spread)
        key_gram = jnp.einsum("chd,jhd->hcj", key_block, key_block, precision=highest)
        lower_part = jnp.where(strict_lower, beta_block.T[:, :, None] * decay_table * key_gram, 0.0)
        system = identity_block + lower_part
        growth = jnp.exp(cumul_heads)
        projected = jnp.einsum("chd,hrd->hcr", key_block, carried, precision=highest)
        right_side = -(beta_block.T * growth)[:, :, None] * projected
        written = jnp.einsum("ch,chv->hcv", beta_block, value_block, precision=highest)
        right_side = jnp.concatenate(
            [right_side[..., :split_at], right_side[..., split_at:] + written], -1
        )
        errors = jax.vmap(
            lambda mat, rhs_part: jax.scipy.linalg.solve_triangular(
                mat, rhs_part, lower=True, unit_diagonal=True
            )
        )(system, right_side)
        last_log = cumul_heads[:, -1]
        weights = jnp.exp(last_log[None, :] - cumulative)
        updated = jnp.exp(last_log)[:, None, None] * carried + jnp.einsum(
            "hcr,chd->hrd", errors, key_block * weights[:, :, None], precision=highest
        )
        emitted = None
        if with_output:
            carried_term = jnp.einsum("chd,hvd->chv", query_block, carried, precision=highest)
            scores = jnp.einsum("chd,jhd->hcj", query_block, key_block, precision=highest)
            masked_scores = jnp.where(inclusive, scores * decay_table, 0.0)
            emitted = growth.T[:, :, None] * carried_term + jnp.einsum(
                "hcj,hjv->chv", masked_scores, errors, precision=highest
            )
        return (updated, emitted)

    def blocked(source):
        return source.reshape((block_count, BLK) + source.shape[1:])

    query_src = key_unit if queries is None else queries
    final_pairs, emitted_all = lax.scan(
        advance,
        initial,
        (
            blocked(key_unit),
            blocked(query_src),
            blocked(values),
            blocked(beta_vals),
            blocked(gate_logs),
        ),
    )
    if with_output:
        emitted_all = emitted_all.reshape(total_rows, head_count, DV)
    return (final_pairs, emitted_all)


def compose(earlier, later):
    highest = lax.Precision.HIGHEST
    joined_transition = jnp.einsum("hij,hjk->hik", earlier[0], later[0], precision=highest)
    joined_offset = jnp.einsum("hij,hjk->hik", earlier[1], later[0], precision=highest) + later[1]
    return (joined_transition, joined_offset)


def local(query_rows, key_rows, value_rows, beta_rows, log_gate):
    query_here, key_here, value_here, beta_here, gate_here = (
        lax.all_to_all(query_rows, "head", split_axis=1, concat_axis=0, tiled=True),
        lax.all_to_all(key_rows, "head", split_axis=1, concat_axis=0, tiled=True),
        lax.all_to_all(value_rows, "head", split_axis=1, concat_axis=0, tiled=True),
        lax.all_to_all(beta_rows, "head", split_axis=1, concat_axis=0, tiled=True),
        lax.all_to_all(log_gate, "head", split_axis=1, concat_axis=0, tiled=True),
    )
    group_ratio = VALUE_HEADS // HK
    key_unit = jnp.repeat(unit_rows(key_here), group_ratio, axis=1)
    values = value_here.astype(jnp.float32)
    beta_vals = beta_here.astype(jnp.float32)
    gate_logs = gate_here.astype(jnp.float32)
    head_count = values.shape[1]
    start_pairs = jnp.concatenate(
        [
            jnp.broadcast_to(jnp.eye(DK, dtype=jnp.float32), (head_count, DK, DK)),
            jnp.zeros((head_count, DV, DK), jnp.float32),
        ],
        1,
    )
    final_pairs, unused_rows = sweep_blocks(
        start_pairs, key_unit, None, values, beta_vals, gate_logs, False
    )
    transition = final_pairs[:, :DK]
    offset = final_pairs[:, DK:]
    identity_pair = (
        jnp.broadcast_to(jnp.eye(DK, dtype=jnp.float32), (head_count, DK, DK)),
        jnp.zeros((head_count, DV, DK), jnp.float32),
    )
    unused_transition, incoming = entering((transition, offset), "ctx", compose, identity_pair)
    query_unit = jnp.repeat(unit_rows(query_here), group_ratio, axis=1) * DK ** (-0.5)
    unused_final, result = sweep_blocks(
        incoming, key_unit, query_unit, values, beta_vals, gate_logs, True
    )
    return lax.all_to_all(
        result.astype(jnp.bfloat16), "head", split_axis=0, concat_axis=1, tiled=True
    )


def solution(mesh):
    placed = (
        P(("ctx", "head"), None, None),
        P(("ctx", "head"), None, None),
        P(("ctx", "head"), None, None),
        P(("ctx", "head"), None),
        P(("ctx", "head"), None),
    )
    return jax.shard_map(
        local, mesh=mesh, in_specs=placed, out_specs=P(("ctx", "head"), None, None), check_vma=False
    )
```

profile of v0, /device:TPU:1, one launch (start us, length us, event | category | flops | bytes accessed | tf_op | source)
XLA Modules:
  0.0 1150.3 jit_solution(8263468970713126694)
XLA Ops:
  6.5 11.2 all_to_all.71
  17.8 3.9 all-to-all-start.1
  21.7 2.0 copy.170
  23.7 2.7 all-to-all-done.1
  26.3 4.1 all-to-all-start.2
  31.9 8.0 all-to-all-done.2
  39.9 5.0 all-to-all-start.3
  47.1 13.0 %all-to-all-done.3 = bf16[128,32,128]{2,0,1:T(8,128)(2,1)} async-done(((bf16[128,32,128]{2,0,1:T(8,128)(2,1)}), bf16[128,32,128]{2,0,1:T(8,128)(2,1)}, u32[]{:S(2)}, u32[]{:S(2)}) %all-to-all-start.3) | async-done | bytes 1048608 | tf_op jit(solution)/shard_map/all_to_all | solution.py:110
  60.1 2.8 convert_bitcast_fusion
  62.9 379.3 %while.38 = (s32[]{:T(128)}, f32[4,256,128]{2,1,0:T(8,128)S(1)}, f32[8,128,4]{2,1,0:T(8,128)}, f32[8,128,4]{1,2,0:T(4,128)S(1)}, f32[8,128,4,128]{3,1,2,0:T(8,12...) while((s32[]{:T(128)}, f32[4,256,128]{2,1,0:T(8,128)S(1)}, f32[8,128,4]{2,1,0:T(8,128)}, ...), condition=%wide.region_3.4_spmd.clone, body=%wide.region_1.3_spmd.clone.sunk | while | flops 706053248 | bytes 6661825 | solution.py:83
  64.6 1.8 fusion.125
  67.3 39.9 %custom-call.14 = f32[4,1,128,128]{2,3,1,0:T(8,128)} custom-call(f32[4,1,128,128]{3,2,1,0:T(8,128)S(1)} %fusion.127), custom_call_target="InvertDiagBlocksLowerTriangular" | custom-call | tf_op jit(solution)/shard_map/while/body/eval_jaxpr/vmap(jit(_solve_triangular))/triangular_solve | solution.py:60
  107.2 2.1 fusion.128
  112.1 1.8 fusion.125
  114.7 39.9 %custom-call.14 = f32[4,1,128,128]{2,3,1,0:T(8,128)} custom-call(f32[4,1,128,128]{3,2,1,0:T(8,128)S(1)} %fusion.127), custom_call_target="InvertDiagBlocksLowerTriangular" | custom-call | tf_op jit(solution)/shard_map/while/body/eval_jaxpr/vmap(jit(_solve_triangular))/triangular_solve | solution.py:60
  154.6 2.1 fusion.128
  159.5 1.8 fusion.125
  162.1 39.9 %custom-call.14 = f32[4,1,128,128]{2,3,1,0:T(8,128)} custom-call(f32[4,1,128,128]{3,2,1,0:T(8,128)S(1)} %fusion.127), custom_call_target="InvertDiagBlocksLowerTriangular" | custom-call | tf_op jit(solution)/shard_map/while/body/eval_jaxpr/vmap(jit(_solve_triangular))/triangular_solve | solution.py:60
  202.0 2.1 fusion.128
  209.5 39.9 %custom-call.14 = f32[4,1,128,128]{2,3,1,0:T(8,128)} custom-call(f32[4,1,128,128]{3,2,1,0:T(8,128)S(1)} %fusion.127), custom_call_target="InvertDiagBlocksLowerTriangular" | custom-call | tf_op jit(solution)/shard_map/while/body/eval_jaxpr/vmap(jit(_solve_triangular))/triangular_solve | solution.py:60
  249.5 2.1 fusion.128
  256.9 39.9 %custom-call.14 = f32[4,1,128,128]{2,3,1,0:T(8,128)} custom-call(f32[4,1,128,128]{3,2,1,0:T(8,128)S(1)} %fusion.127), custom_call_target="InvertDiagBlocksLowerTriangular" | custom-call | tf_op jit(solution)/shard_map/while/body/eval_jaxpr/vmap(jit(_solve_triangular))/triangular_solve | solution.py:60
  296.9 2.1 fusion.128
  301.7 1.8 fusion.125
  304.4 39.9 %custom-call.14 = f32[4,1,128,128]{2,3,1,0:T(8,128)} custom-call(f32[4,1,128,128]{3,2,1,0:T(8,128)S(1)} %fusion.127), custom_call_target="InvertDiagBlocksLowerTriangular" | custom-call | tf_op jit(solution)/shard_map/while/body/eval_jaxpr/vmap(jit(_solve_triangular))/triangular_solve | solution.py:60
  344.3 2.1 fusion.128
  351.8 39.9 %custom-call.14 = f32[4,1,128,128]{2,3,1,0:T(8,128)} custom-call(f32[4,1,128,128]{3,2,1,0:T(8,128)S(1)} %fusion.127), custom_call_target="InvertDiagBlocksLowerTriangular" | custom-call | tf_op jit(solution)/shard_map/while/body/eval_jaxpr/vmap(jit(_solve_triangular))/triangular_solve | solution.py:60
  391.7 2.1 fusion.128
  399.2 39.9 %custom-call.14 = f32[4,1,128,128]{2,3,1,0:T(8,128)} custom-call(f32[4,1,128,128]{3,2,1,0:T(8,128)S(1)} %fusion.127), custom_call_target="InvertDiagBlocksLowerTriangular" | custom-call | tf_op jit(solution)/shard_map/while/body/eval_jaxpr/vmap(jit(_solve_triangular))/triangular_solve | solution.py:60
  439.1 2.1 fusion.128
  443.9 2.0 copy.177
  445.8 4.3 all-to-all-start.4
  450.1 9.5 all-to-all-done.4
  461.5 80.3 %all-gather.5.cloned.1.call-done = f32[128,128,128]{2,1,0:T(8,128)} async-done(((f32[4,128,128]{2,1,0:T(8,128)}), f32[128,128,128]{2,1,0:T(8,128)}) %all-gather.5.cloned.1.call-update) | async-done | bytes 8388624 | tf_op jit(solution)/shard_map/all_gather | solution.py:15
  541.8 98.0 %all-gather.7.cloned.1.call-done = f32[128,128,128]{2,1,0:T(8,128)} async-done(((f32[4,128,128]{2,1,0:T(8,128)}), f32[128,128,128]{2,1,0:T(8,128)}) %all-gather.7.cloned.1.call-update) | async-done | bytes 8388624 | tf_op jit(solution)/shard_map/all_gather | solution.py:15
  639.8 84.6 %while.40 = (s32[]{:T(128)}, f32[4,128,128]{1,2,0:T(8,128)S(1)}, s32[]{:T(128)}, f32[32,4,128,128]{3,2,1,0:T(8,128)}, f32[32,4,128,128]{3,2,1,0:T(8,128)}, /*index=5*/s32[]{:T(128)}, s32[]{:T(128)}) while((s32[]{:T(128)}, f32[4,128,128]{1,2,0:T(8,128)S(1)}, s32[]{:T(128)}, f32[32,4,128,128]{3,2,1,0:T(8,128)}, ...), condition=%wide.region_5.6_spmd.clone, body=%wide.region_4.5_spmd.clone.sunk | while | flops 100925440 | bytes 2885731 | solution.py:24
  724.6 2.7 broadcast_in_dim.35
  727.3 392.0 %while.39 = (s32[]{:T(128)}, f32[4,128,128]{2,1,0:T(8,128)S(1)}, bf16[8,128,4,128]{3,1,0,2:T(8,128)(2,1)}, f32[8,128,4]{2,1,0:T(8,128)}, f32[8,128,4]{1,2,0:T(4,...) while((s32[]{:T(128)}, f32[4,128,128]{2,1,0:T(8,128)S(1)}, ...), condition=%wide.region_9.10_spmd.clone, body=%wide.region_7.9_spmd.clone.sunk | while | flops 706135168 | bytes 6447817 | solution.py:83
  729.2 39.3 %custom-call.15 = f32[4,1,128,128]{2,3,1,0:T(8,128)S(1)} custom-call(f32[4,1,128,128]{3,2,1,0:T(8,128)S(1)} %fusion.143), custom_call_target="InvertDiagBlocksLowerTriangular" | custom-call | tf_op jit(solution)/shard_map/while/body/eval_jaxpr/vmap(jit(_solve_triangular))/triangular_solve | solution.py:60
  778.2 39.3 %custom-call.15 = f32[4,1,128,128]{2,3,1,0:T(8,128)S(1)} custom-call(f32[4,1,128,128]{3,2,1,0:T(8,128)S(1)} %fusion.143), custom_call_target="InvertDiagBlocksLowerTriangular" | custom-call | tf_op jit(solution)/shard_map/while/body/eval_jaxpr/vmap(jit(_solve_triangular))/triangular_solve | solution.py:60
  827.2 39.3 %custom-call.15 = f32[4,1,128,128]{2,3,1,0:T(8,128)S(1)} custom-call(f32[4,1,128,128]{3,2,1,0:T(8,128)S(1)} %fusion.143), custom_call_target="InvertDiagBlocksLowerTriangular" | custom-call | tf_op jit(solution)/shard_map/while/body/eval_jaxpr/vmap(jit(_solve_triangular))/triangular_solve | solution.py:60
  876.2 39.3 %custom-call.15 = f32[4,1,128,128]{2,3,1,0:T(8,128)S(1)} custom-call(f32[4,1,128,128]{3,2,1,0:T(8,128)S(1)} %fusion.143), custom_call_target="InvertDiagBlocksLowerTriangular" | custom-call | tf_op jit(solution)/shard_map/while/body/eval_jaxpr/vmap(jit(_solve_triangular))/triangular_solve | solution.py:60
  925.2 39.3 %custom-call.15 = f32[4,1,128,128]{2,3,1,0:T(8,128)S(1)} custom-call(f32[4,1,128,128]{3,2,1,0:T(8,128)S(1)} %fusion.143), custom_call_target="InvertDiagBlocksLowerTriangular" | custom-call | tf_op jit(solution)/shard_map/while/body/eval_jaxpr/vmap(jit(_solve_triangular))/triangular_solve | solution.py:60
  974.2 39.3 %custom-call.15 = f32[4,1,128,128]{2,3,1,0:T(8,128)S(1)} custom-call(f32[4,1,128,128]{3,2,1,0:T(8,128)S(1)} %fusion.143), custom_call_target="InvertDiagBlocksLowerTriangular" | custom-call | tf_op jit(solution)/shard_map/while/body/eval_jaxpr/vmap(jit(_solve_triangular))/triangular_solve | solution.py:60
  1023.2 39.3 %custom-call.15 = f32[4,1,128,128]{2,3,1,0:T(8,128)S(1)} custom-call(f32[4,1,128,128]{3,2,1,0:T(8,128)S(1)} %fusion.143), custom_call_target="InvertDiagBlocksLowerTriangular" | custom-call | tf_op jit(solution)/shard_map/while/body/eval_jaxpr/vmap(jit(_solve_triangular))/triangular_solve | solution.py:60
  1072.2 39.3 %custom-call.15 = f32[4,1,128,128]{2,3,1,0:T(8,128)S(1)} custom-call(f32[4,1,128,128]{3,2,1,0:T(8,128)S(1)} %fusion.143), custom_call_target="InvertDiagBlocksLowerTriangular" | custom-call | tf_op jit(solution)/shard_map/while/body/eval_jaxpr/vmap(jit(_solve_triangular))/triangular_solve | solution.py:60
  1119.2 2.0 copy.184
  1121.3 20.2 %all_to_all.72 = bf16[1024,4,128]{2,1,0:T(4,128)(2,1)S(1)} all-to-all(bf16[1024,4,128]{2,1,0:T(4,128)(2,1)S(1)} %copy.184), channel_id=1, replica_groups=mesh['ctx'=32,'head'=8] {'head'}, dimensions={0} | all-to-all | bytes 2097152 | tf_op jit(solution)/shard_map/all_to_all | solution.py:141
  (432 shorter events, 204.3 us)
Async XLA Ops:
  6.5 23.9 %copy-start = (bf16[128,32,128]{2,1,0:T(8,128)(2,1)S(1)}, bf16[128,32,128]{2,1,0:T(8,128)(2,1)}, u32[]{:S(2)}) copy-start(bf16[128,32,128]{2,1,0:T(8,128)(2,1)} %param.13) | copy-start | bytes 3145732
  17.8 8.6 all-to-all-start.1
  26.3 13.6 %all-to-all-start.2 = ((bf16[128,16,128]{2,0,1:T(8,128)(2,1)}), bf16[128,16,128]{2,0,1:T(8,128)(2,1)S(1)}, u32[]{:S(2)}, u32[]{:S(2)}) async-start(bf16[128,16,128]{2,0,1:T(8,128)(2,1)} %copy.170), calls=%async_computation.2 | async-start | bytes 1048576 | tf_op jit(solution)/shard_map/all_to_all | solution.py:109
  39.9 20.2 %all-to-all-start.3 = ((bf16[128,32,128]{2,0,1:T(8,128)(2,1)}), bf16[128,32,128]{2,0,1:T(8,128)(2,1)}, u32[]{:S(2)}, u32[]{:S(2)}) async-start(bf16[128,32,128]{2,0,1:T(8,128)(2,1)} %copy.172), calls=%async_computation.3 | async-start | bytes 2097152 | tf_op jit(solution)/shard_map/all_to_all | solution.py:110
  44.9 496.9 %all-gather.5.cloned.1.call-start = ((), (), s32[]{:S(2)}) async-start(), calls=%async_computation.6 | async-start | bytes 8650752 | tf_op jit(solution)/shard_map/all_gather | solution.py:15
  443.1 196.7 %all-gather.7.cloned.1.call-start = ((), (), s32[]{:S(2)}) async-start(), calls=%async_computation.7 | async-start | bytes 8650752 | tf_op jit(solution)/shard_map/all_gather | solution.py:15
  445.8 13.8 %all-to-all-start.4 = ((bf16[128,16,128]{2,0,1:T(8,128)(2,1)}), bf16[128,16,128]{2,0,1:T(8,128)(2,1)S(1)}, u32[]{:S(2)}, u32[]{:S(2)}) async-start(bf16[128,16,128]{2,0,1:T(8,128)(2,1)} %copy.177), calls=%async_computation.4 | async-start | bytes 1048576 | tf_op jit(solution)/shard_map/all_to_all | solution.py:108
Sparse Core Ops, SparseCore 0:
  443.2 98.5 all-gather.4
  544.4 95.4 all-gather.6
where the time goes:
time: 1150 us
  other arithmetic  659 us (57%)
  waiting for transfers between devices  212 us (18%)
  matrix products  146 us (13%)
  local copies, waits for them, and re-layouts  68.1 us (6%)
  blocking collectives  31.4 us (3%)
  starting transfers between devices  17.3 us (2%)
  between operations  13.6 us (1%)
    another operation x48, other arithmetic, advance(): jax.scipy.linalg.solve_triangular(mat, rhs_part, lower=True, unit_diagona...  634 us
    all_gather x2, waiting for transfers between devices, entering(): pieces = jax.tree.map(lambda part: lax.all_gather(part, axis), value)  178 us
    dot_general x31, matrix products, compose(): jnp.einsum('hij,hjk->hik', earlier[1], later[0], precision=highest)  48.4 us
    dynamic_slice x62, local copies, waits for them, and re-layouts, step(): longer = join(subtotal, jax.tree.map(lambda part: part[position], pieces))  34.1 us
  transfers between devices with their start and end apart: 6, of which 6 were waited for; matrix products, arithmetic and copies ran while one was open for 1% of the time, Pallas kernels for 0%

commit v1 on v0

v1 whole, which is shorter than its diff:
```python
import jax
import jax.numpy as jnp
from jax import lax
from jax.experimental import pallas as pl
from jax.experimental.pallas import tpu as pltpu
from jax.sharding import PartitionSpec as P

N = 128
HEADS = 4
KEYS = 2
BLOCKS = 8
ROWS = 1040
Q0, V0, G0 = KEYS * N, 2 * KEYS * N, 2 * KEYS * N + HEADS * N
STEP = 2
F32, BF16 = jnp.float32, jnp.bfloat16


def iota(shape, dim):
    return lax.broadcasted_iota(jnp.int32, shape, dim)


def split(x):
    hi = x.astype(BF16)
    return hi, (x - hi.astype(F32)).astype(BF16)


def dot(a, b):
    return jnp.dot(a, b, preferred_element_type=F32)


def dot_nt(a, b):
    return lax.dot_general(a, b, (((1,), (1,)), ((), ())), preferred_element_type=F32)


def dot_tn(a, b):
    return lax.dot_general(a, b, (((0,), (0,)), ((), ())), preferred_element_type=F32)


def left(a):
    hi, lo = a
    return jnp.concatenate([hi, lo, hi, lo], axis=1)


def right(b):
    hi, lo = b
    return jnp.concatenate([hi, hi, lo, lo], axis=0)


def dot4(a, b):
    return dot(left(a), right(b))


def gate_rows(gates):
    upper = (iota((N, N), 0) <= iota((N, N), 1)).astype(F32).astype(BF16)
    return dot(gates, upper)


def gate_columns(gates):
    lower = (iota((N, N), 0) >= iota((N, N), 1)).astype(F32).astype(BF16)
    eye = (iota((N, N), 0) == iota((N, N), 1)).astype(F32).astype(BF16)
    both = dot_nt(jnp.concatenate([lower, eye], axis=0), gates)
    return both[:N], both[N:]


def small_inverses(lower_parts):
    count = len(lower_parts)
    group = iota((16, N), 1) // 16
    rows = []
    for part in lower_parts:
        packed = jnp.zeros((16, N), F32)
        for b in range(8):
            packed = jnp.where(group == b, part[16 * b : 16 * b + 16], packed)
        rows.append(packed)
    packed = jnp.concatenate(rows, axis=0)
    lane = iota((16 * count, N), 1)
    result = (lane % 16 == iota((16 * count, N), 0) % 16).astype(F32).reshape(count, 16, N)
    for j in range(15):
        factor = jnp.take_along_axis(packed, lane // 16 * 16 + j, axis=1).reshape(count, 16, N)
        result = result - factor * result[:, j : j + 1, :]
    return [
        jnp.concatenate([jnp.where(group == b, result[c], 0.0) for b in range(8)], axis=0)
        for c in range(count)
    ]


def merge(inverse, lower_part, size):
    starts = range(size, N, 2 * size)

    def pick(x):
        return jnp.concatenate([x[s : s + size] for s in starts], axis=0)

    half = (N // 2, N)
    row_pair = iota(half, 0) // size
    link = jnp.where(iota(half, 1) // size == 2 * row_pair, pick(lower_part), 0.0)
    hi, lo = split(inverse)
    linked = split(dot4(split(link), (hi, lo)))

    def spread(x):
        zero = jnp.zeros((size, N), BF16)
        pieces = []
        for p in range(len(starts)):
            pieces += [zero, x[p * size : (p + 1) * size]]
        return jnp.concatenate(pieces, axis=0)

    picked = pick(inverse)
    new = picked - dot4((pick(hi), pick(lo)), (spread(linked[0]), spread(linked[1])))
    pieces = []
    for p, s in enumerate(starts):
        pieces += [inverse[s - size : s], new[p * size : (p + 1) * size]]
    return jnp.concatenate(pieces, axis=0)


def blocks_kernel(x_ref, wu_ref, ph_ref, aux_ref, pair_ref, state):
    step = pl.program_id(0)
    eye = iota((N, N), 0) == iota((N, N), 1)
    strict = iota((N, N), 0) > iota((N, N), 1)

    @pl.when(step == 0)
    def _():
        start = (iota((N, 2 * N), 0) == iota((N, 2 * N), 1)).astype(F32)
        for h in range(HEADS):
            state[h] = start

    lower_parts, scales, keys = [], [], []
    for b in range(STEP):
        gates = x_ref[b, G0 : G0 + 16]
        cumulative_row = gate_rows(gates)
        cumulative_col, beta_col = gate_columns(gates)
        beta_row = gates.astype(F32)
        norm_rows = []
        for kh in range(KEYS):
            key = x_ref[b, kh * N : (kh + 1) * N]
            gram = dot_nt(key, key)
            diagonal = jnp.where(eye, gram, 0.0)
            norm_row = lax.rsqrt(jnp.sum(diagonal, axis=0, keepdims=True) + 1e-06)
            norm_col = lax.rsqrt(jnp.sum(diagonal, axis=1, keepdims=True) + 1e-06)
            norm_rows.append(norm_row)
            gram = jnp.where(strict, gram * norm_col * norm_row, 0.0)
            for h in range(2 * kh, 2 * kh + 2):
                crow = cumulative_row[4 + h : 5 + h]
                ccol = cumulative_col[:, 4 + h : 5 + h]
                decay = jnp.exp(jnp.minimum(ccol - crow, 0.0))
                lower_parts.append(gram * decay * beta_col[:, h : h + 1])
                last = crow[:, N - 1 : N]
                brow = beta_row[h : h + 1]
                scales.append((
                    brow * jnp.exp(crow) * norm_row,
                    brow,
                    norm_col * jnp.exp(last - ccol),
                    jnp.exp(last),
                ))
                keys.append((b, kh, h))
        aux_ref[b] = jnp.concatenate([cumulative_row[4:8]] + norm_rows + [jnp.zeros((2, N), F32)], axis=0)
    inverses = small_inverses(lower_parts)
    for size in (16, 32, 64):
        inverses = [merge(t, g, size) for t, g in zip(inverses, lower_parts)]
    transitions = []
    for inverse, (for_w, for_u, for_state, last), (b, kh, h) in zip(inverses, scales, keys):
        key = x_ref[b, kh * N : (kh + 1) * N]
        value = x_ref[b, V0 + h * N : V0 + (h + 1) * N]
        w = dot(jnp.concatenate(split(inverse * for_w), axis=1), jnp.concatenate([key, key], axis=0))
        u = dot(jnp.concatenate(split(inverse * for_u), axis=1), jnp.concatenate([value, value], axis=0))
        wu = jnp.concatenate([w, u], axis=1)
        wu_ref[b, h] = wu
        ab = dot_tn(
            jnp.concatenate([key, key], axis=0), jnp.concatenate(split(wu * for_state), axis=0)
        )
        transitions.append((
            left(split(jnp.where(eye, last, 0.0) - ab[:, :N])),
            ab[:, N:],
        ))
    for (a, offset), (b, kh, h) in zip(transitions, keys):
        hi, lo = split(state[h])
        ph_ref[b, h] = jnp.concatenate([hi, lo], axis=0)
        moved = dot(a, right((hi, lo)))
        state[h, :, :N] = moved[:, :N]
        state[h, :, N:] = moved[:, N:] + offset

    @pl.when(step == pl.num_programs(0) - 1)
    def _():
        for h in range(HEADS):
            pair_ref[h, :N] = state[h, :, :N].T
            pair_ref[h, N:] = state[h, :, N:].T


def blocks(x):
    steps = BLOCKS // STEP
    return pl.pallas_call(
        blocks_kernel,
        grid=(steps,),
        in_specs=[pl.BlockSpec((STEP, ROWS, N), lambda i: (i, 0, 0))],
        out_specs=[
            pl.BlockSpec((STEP, HEADS, N, 2 * N), lambda i: (i, 0, 0, 0)),
            pl.BlockSpec((STEP, HEADS, 2 * N, 2 * N), lambda i: (i, 0, 0, 0)),
            pl.BlockSpec((STEP, 8, N), lambda i: (i, 0, 0)),
            pl.BlockSpec((HEADS, 2 * N, N), lambda i: (0, 0, 0)),
        ],
        out_shape=[
            jax.ShapeDtypeStruct((BLOCKS, HEADS, N, 2 * N), F32),
            jax.ShapeDtypeStruct((BLOCKS, HEADS, 2 * N, 2 * N), BF16),
            jax.ShapeDtypeStruct((BLOCKS, 8, N), F32),
            jax.ShapeDtypeStruct((HEADS, 2 * N, N), F32),
        ],
        scratch_shapes=[pltpu.VMEM((HEADS, N, 2 * N), F32)],
        compiler_params=pltpu.CompilerParams(
            dimension_semantics=("arbitrary",), vmem_limit_bytes=48 * 2**20
        ),
        cost_estimate=pl.CostEstimate(flops=10**9, bytes_accessed=10 * 2**20, transcendentals=10**6),
        name="blocks",
    )(x)


def rows_kernel(x_ref, wu_ref, ph_ref, aux_ref, r_ref, o_ref):
    inclusive = iota((N, N), 0) >= iota((N, N), 1)
    gates = x_ref[0, G0 : G0 + 16]
    cumulative_col, _ = gate_columns(gates)
    for kh in range(KEYS):
        key = x_ref[0, kh * N : (kh + 1) * N]
        query = x_ref[0, Q0 + kh * N : Q0 + (kh + 1) * N]
        wide = query.astype(F32)
        norm = lax.rsqrt(jnp.sum(wide * wide, axis=1, keepdims=True) + 1e-06) * N ** (-0.5)
        unit = wide * norm
        scores = dot_nt(query, key) * norm * aux_ref[0, 4 + kh : 5 + kh]
        scores = jnp.where(inclusive, scores, 0.0)
        for h in range(2 * kh, 2 * kh + 2):
            ccol = cumulative_col[:, 4 + h : 5 + h]
            decay = jnp.exp(jnp.minimum(ccol - aux_ref[0, h : h + 1], 0.0))
            inner = dot4(split(scores * decay), split(wu_ref[0, h]))
            reach = split(unit * jnp.exp(ccol) - inner[:, :N])
            ph = ph_ref[0, h]
            both = dot(left(reach), right((ph[:N], ph[N:])))
            r_ref[0, h] = jnp.concatenate(split(both[:, :N]), axis=1)
            o_ref[0, h] = both[:, N:] + inner[:, N:]


def rows(x, wu, ph, aux):
    def spec(*shape):
        return pl.BlockSpec((1,) + shape, lambda i: (i,) + (0,) * len(shape))

    return pl.pallas_call(
        rows_kernel,
        grid=(BLOCKS,),
        in_specs=[spec(ROWS, N), spec(HEADS, N, 2 * N), spec(HEADS, 2 * N, 2 * N), spec(8, N)],
        out_specs=[spec(HEADS, N, 2 * N), spec(HEADS, N, N)],
        out_shape=[
            jax.ShapeDtypeStruct((BLOCKS, HEADS, N, 2 * N), BF16),
            jax.ShapeDtypeStruct((BLOCKS, HEADS, N, N), F32),
        ],
        compiler_params=pltpu.CompilerParams(
            dimension_semantics=("arbitrary",), vmem_limit_bytes=32 * 2**20
        ),
        cost_estimate=pl.CostEstimate(flops=2 * 10**9, bytes_accessed=14 * 2**20, transcendentals=10**6),
        name="rows",
    )(x, wu, ph, aux)


def prefix_kernel(pairs_ref, prefix_ref, total_ref):
    width = N + N // 2
    prefix_ref[0] = jnp.where(iota((width, N), 0) == iota((width, N), 1), 1.0, 0.0)
    running = pairs_ref[0]
    for s in range(1, 8):
        prefix_ref[s] = running
        nxt = pairs_ref[s]
        running = dot4(split(running), split(nxt[:N]))
        running = running + jnp.concatenate([jnp.zeros((N, N), F32), nxt[N:]], axis=0)
    total_ref[...] = running


def prefix(pairs):
    width = N + N // 2
    return pl.pallas_call(
        prefix_kernel,
        out_shape=[
            jax.ShapeDtypeStruct((8, width, N), F32),
            jax.ShapeDtypeStruct((width, N), F32),
        ],
        name="prefix",
    )(pairs)


def incoming_kernel(group_ref, prefix_ref, g1_ref, g2_ref, g3_ref, out_ref):
    group = group_ref[0]
    others = (g1_ref, g2_ref, g3_ref)
    state = jnp.zeros((N // 2, N), F32)
    for back in (3, 2, 1):
        other = others[back - 1]
        moved = dot4(split(state), split(other[:N])) + other[N:]
        state = jnp.where(back <= group, moved, state)
    state = left(split(state))
    for s in range(8):
        out_ref[s] = dot(state, right(split(prefix_ref[s, :N]))) + prefix_ref[s, N:]


def incoming(group, prefixes, others):
    vmem = pl.BlockSpec(memory_space=pltpu.VMEM)
    return pl.pallas_call(
        incoming_kernel,
        in_specs=[pl.BlockSpec(memory_space=pltpu.SMEM)] + [vmem] * 4,
        out_shape=jax.ShapeDtypeStruct((8, N // 2, N), F32),
        name="incoming",
    )(group, prefixes, *others)


def finish_kernel(r_ref, o_ref, s_ref, out_ref, state):
    @pl.when(pl.program_id(0) == 0)
    def _():
        for h in range(HEADS):
            hi, lo = split(s_ref[h])
            state[h] = jnp.concatenate([hi, hi, lo, lo], axis=1)

    for h in range(HEADS):
        r = r_ref[0, h]
        out = dot_nt(jnp.concatenate([r, r], axis=1), state[h]) + o_ref[0, h]
        out_ref[0, h] = out.astype(BF16)


def finish(r, o, s):
    def spec(*shape):
        return pl.BlockSpec((1,) + shape, lambda i: (i,) + (0,) * len(shape))

    return pl.pallas_call(
        finish_kernel,
        grid=(BLOCKS,),
        in_specs=[
            spec(HEADS, N, 2 * N),
            spec(HEADS, N, N),
            pl.BlockSpec((HEADS, N, N), lambda i: (0, 0, 0)),
        ],
        out_specs=spec(HEADS, N, N),
        out_shape=jax.ShapeDtypeStruct((BLOCKS, HEADS, N, N), BF16),
        scratch_shapes=[pltpu.VMEM((HEADS, N, 4 * N), BF16)],
        compiler_params=pltpu.CompilerParams(dimension_semantics=("arbitrary",)),
        name="finish",
    )(r, o, s)


def pack(query_rows, key_rows, value_rows, beta_rows, log_gate):
    def by_owner(x):
        owned = x.reshape(N, 8, -1, N).transpose(1, 2, 0, 3)
        return owned.reshape(8, -1, N)

    def gates(x):
        return x.T.reshape(8, HEADS, N)

    fill = jnp.zeros((8, ROWS - G0 - 2 * HEADS, N), BF16)
    return jnp.concatenate(
        [
            by_owner(key_rows),
            by_owner(query_rows),
            by_owner(value_rows),
            gates(beta_rows),
            gates(log_gate),
            fill,
        ],
        axis=1,
    )


EIGHTS = [list(range(8 * g, 8 * g + 8)) for g in range(4)]


def states_before(pair):
    half = N // 2
    a = jnp.broadcast_to(pair[:, None, :N], (HEADS, 2, N, N))
    b = pair[:, N:].reshape(HEADS, 2, half, N)
    send = jnp.concatenate([a, b], axis=2).reshape(8, N + half, N)
    got = lax.all_to_all(send, "ctx", 0, 0, tiled=True, axis_index_groups=EIGHTS)
    prefixes, total = prefix(got)
    others = []
    for back in (1, 2, 3):
        ring = [(i, (i + 8 * back) % 32) for i in range(32)]
        others.append(lax.ppermute(total, "ctx", ring))
    group = (lax.axis_index("ctx") // 8).astype(jnp.int32).reshape(1)
    states = incoming(group, prefixes, others)
    mine = lax.all_to_all(states, "ctx", 0, 0, tiled=True, axis_index_groups=EIGHTS)
    return mine.reshape(HEADS, N, N)


def local(query_rows, key_rows, value_rows, beta_rows, log_gate):
    packed = pack(query_rows, key_rows, value_rows, beta_rows, log_gate)
    x = lax.all_to_all(packed, "head", 0, 0, tiled=True)
    wu, ph, aux, pair = blocks(x)
    state = states_before(pair)
    r, o = rows(x, wu, ph, aux)
    out = finish(r, o, state)
    back = lax.all_to_all(out, "head", 0, 0, tiled=True)
    return back.reshape(8 * HEADS, N, N).transpose(1, 0, 2)


def solution(mesh):
    placed = (
        P(("ctx", "head"), None, None),
        P(("ctx", "head"), None, None),
        P(("ctx", "head"), None, None),
        P(("ctx", "head"), None),
        P(("ctx", "head"), None),
    )
    return jax.shard_map(
        local, mesh=mesh, in_specs=placed, out_specs=P(("ctx", "head"), None, None), check_vma=False
    )
```

time: 1150 us -> 160 us (0.14)
  other arithmetic: 659 us -> 0.05 us
  waiting for transfers between devices: 212 us -> 3.86 us
  matrix products: 146 us -> 0 us
  Pallas kernels: 0 us -> 50.6 us
  local copies, waits for them, and re-layouts: 68.1 us -> 19 us
  blocking collectives: 31.4 us -> 71.5 us
  between operations: 13.6 us -> 0.12 us
    another operation x64 -> x0, other arithmetic: 637 us -> none  [the longest x48 634 us: advance(): jax.scipy.linalg.solve_triangular(mat, rhs_part, lower=True, unit_diagona...]
    all_gather x2 -> x0, waiting for transfers between devices: 178 us -> none  [entering(): pieces = jax.tree.map(lambda part: lax.all_gather(part, axis), value)]
    dot_general x103 -> x0, matrix products: 124 us -> none  [the longest x31 48.4 us: compose(): jnp.einsum('hij,hjk->hik', earlier[1], later[0], precision=highest)]
    pallas_call x0 -> x5, Pallas kernels: none -> 50.6 us  [the longest x1 30.3 us: blocks(): pl.pallas_call(blocks_kernel, grid=(steps,), in_specs=[pl.BlockSpec((STEP...]
    all_to_all x2 -> x3, blocking collectives: 31.4 us -> 71.5 us  [the longest x1 34 us: local(): x = lax.all_to_all(packed, 'head', 0, 0, tiled=True)]
    dynamic_slice x62 -> x0, local copies, waits for them, and re-layouts: 34.1 us -> none  [step(): longer = join(subtotal, jax.tree.map(lambda part: part[position], pieces))]
    all_to_all x4 -> x1, waiting for transfers between devices: 33.2 us -> 0.01 us  [states_before(): lax.all_to_all(states, 'ctx', 0, 0, tiled=True, axis_index_groups=EIGHTS)]
    another operation x16 -> x0, matrix products: 21.3 us -> none  [advance(): jax.scipy.linalg.solve_triangular(mat, rhs_part, lower=True, unit_diagona...]
  transfers between devices with their start and end apart: 6 -> 4, of which waited for: 6 -> 2; matrix products, arithmetic and copies ran while one was open for 1% -> 0% of each run, Pallas kernels for 0% -> 5%
where the time goes in v1:
time: 160 us
  blocking collectives  71.5 us (45%)
  Pallas kernels  50.6 us (32%)
  local copies, waits for them, and re-layouts  19 us (12%)
  starting transfers between devices  14.7 us (9%)
  waiting for transfers between devices  3.86 us (2%)
    all_to_all x1, blocking collectives, local(): x = lax.all_to_all(packed, 'head', 0, 0, tiled=True)  34 us
    pallas_call x1, Pallas kernels, blocks(): pl.pallas_call(blocks_kernel, grid=(steps,), in_specs=[pl.BlockSpec((STEP...  30.3 us
    all_to_all x1, blocking collectives, local(): back = lax.all_to_all(out, 'head', 0, 0, tiled=True)  21.4 us
    all_to_all x1, blocking collectives, states_before(): lax.all_to_all(send, 'ctx', 0, 0, tiled=True, axis_index_groups=EIGHTS)  16.1 us
    ppermute x3, starting transfers between devices, states_before(): others.append(lax.ppermute(total, 'ctx', ring))  9.58 us
    unnamed x24, local copies, waits for them, and re-layouts  8.41 us
    pallas_call x1, Pallas kernels, rows(): pl.pallas_call(rows_kernel, grid=(BLOCKS,), in_specs=[spec(ROWS, N), spec...  7.8 us
    pallas_call x1, Pallas kernels, finish(): pl.pallas_call(finish_kernel, grid=(BLOCKS,), in_specs=[spec(HEADS, N, 2...  7.01 us
  transfers between devices with their start and end apart: 4, of which 2 were waited for; matrix products, arithmetic and copies ran while one was open for 0% of the time, Pallas kernels for 5%

profile of v1, /device:TPU:1, one launch (start us, length us, event | category | flops | bytes accessed | tf_op | source)
XLA Modules:
  0.0 159.8 jit_solution(3588216617647162952)
XLA Ops:
  0.0 0.0 copy-start.5
  0.0 0.0 copy-start.6
  0.0 0.0 copy-start.10
  0.0 0.0 copy-start.11
  0.0 1.7 %copy.8 = bf16[128,8,4,128]{3,0,2,1:T(8,128)(2,1)S(1)} copy(bf16[128,8,4,128]{3,2,1,0:T(4,128)(2,1)} %bitcast.31) | data formatting | bytes 2097152 | tf_op jit(solution)/shard_map/reshape | solution.py:339
  1.7 0.0 copy-done.5
  1.7 0.1 copy.6
  1.9 0.0 copy-done.6
  1.9 0.1 copy.7
  2.1 0.0 copy-done.10
  2.1 0.0 copy-done.11
  2.1 6.9 %concatenate.11 = bf16[8,1040,128]{2,1,0:T(8,128)(2,1)} concatenate(bf16[8,256,128]{2,1,0:T(8,128)(2,1)S(1)} %bitcast.29, bf16[8,256,128]{2,1,0:T(8,128)(2,1)S(1)} %bitcast.30, bf16[8,512,128]{2,1,0:T(8,128)(2,1)S(1)} %bitcast.27, bf16[8,4,128]{2,1,0:T(4,128)(2,1)S(1)} %bitcast.36, bf16[8,4,128]{2,1,0:T(4,128)(2,1)S(1)} %bitcast.37, bf16[8,8,128]{2,1,0:T(8,128)(2,1)S(1)} %broadcast_in_dim.4), dimensions={1} | concatenate | bytes 4259840 | tf_op jit(solution)/shard_map/concatenate | solution.py:346
  8.9 34.0 %all_to_all.20.x_ref = bf16[8,1040,128]{2,1,0:T(8,128)(2,1)S(1)} all-to-all(bf16[8,1040,128]{2,1,0:T(8,128)(2,1)} %concatenate.11), channel_id=1, replica_groups=mesh['ctx'=32,'head'=8] {'head'}, dimensions={0} | all-to-all | bytes 4259840 | tf_op jit(solution)/shard_map/all_to_all | solution.py:381
  43.0 30.3 %blocks.1 = (f32[8,4,128,256]{3,2,1,0:T(8,128)}, bf16[8,4,256,256]{3,2,1,0:T(8,128)(2,1)}, f32[8,8,128]{2,1,0:T(8,128)S(1)}, f32[4,256,128]{2,1,0:T(8,128)S(1)}) custom-call(bf16[8,1040,128]{2,1,0:T(8,128)(2,1)S(1)} %all_to_all.20.x_ref), custom_call_target="tpu_custom_call" | custom-call | flops 1000000000 | bytes 10485760 | tf_op jit(solution)/shard_map/blocks/pallas_call | solution.py:188
  73.4 0.1 pad_maximum_fusion
  73.4 16.1 %all_to_all.21.pairs_ref = f32[8,192,128]{2,1,0:T(8,128)} all-to-all(f32[8,192,128]{2,1,0:T(8,128)S(1)} %pad_maximum_fusion), channel_id=1, replica_groups={{0,8,16,24,32,40,48,56},{64,72,80,88,96,104,112,120},{128,136,144,152,1..., dimensions={0} | all-to-all | bytes 1572864 | tf_op jit(solution)/shard_map/all_to_all | solution.py:367
  89.5 2.9 %prefix.1 = (f32[8,192,128]{2,1,0:T(8,128)}, f32[192,128]{1,0:T(8,128)}) custom-call(f32[8,192,128]{2,1,0:T(8,128)} %all_to_all.21.pairs_ref), custom_call_target="tpu_custom_call" | custom-call | tf_op jit(solution)/shard_map/prefix/pallas_call | solution.py:271
  92.4 3.0 %collective-permute-start = (f32[192,128]{1,0:T(8,128)}, f32[192,128]{1,0:T(8,128)S(1)}, u32[]{:S(2)}, u32[]{:S(2)}) collective-permute-start(f32[192,128]{1,0:T(8,128)} %get-tuple-element.20), channel_id=1, source_target_pairs={{0,64},{8,72},{16,80},{24,88},{32,96},{40,104},{48,112},{56,120},{... | collective-permute-start | bytes 294920 | tf_op jit(solution)/shard_map/ppermute | solution.py:372
  95.4 4.2 %collective-permute-start.1 = (f32[192,128]{1,0:T(8,128)}, f32[192,128]{1,0:T(8,128)S(1)}, u32[]{:S(2)}, u32[]{:S(2)}) collective-permute-start(f32[192,128]{1,0:T(8,128)} %get-tuple-element.20), channel_id=1, source_target_pairs={{0,128},{8,136},{16,144},{24,152},{32,160},{40,168},{48,176},{56,1... | collective-permute-start | bytes 294920 | tf_op jit(solution)/shard_map/ppermute | solution.py:372
  99.6 2.4 %collective-permute-start.2 = (f32[192,128]{1,0:T(8,128)}, f32[192,128]{1,0:T(8,128)S(1)}, u32[]{:S(2)}, u32[]{:S(2)}) collective-permute-start(f32[192,128]{1,0:T(8,128)} %get-tuple-element.20), channel_id=1, source_target_pairs={{0,192},{8,200},{16,208},{24,216},{32,224},{40,232},{48,240},{56,2... | collective-permute-start | bytes 294920 | tf_op jit(solution)/shard_map/ppermute | solution.py:372
  102.0 0.0 collective-permute-done.g1_ref
  102.0 0.0 copy-start.7
  102.0 2.4 %collective-permute-done.1.g2_ref = f32[192,128]{1,0:T(8,128)S(1)} collective-permute-done((f32[192,128]{1,0:T(8,128)}, f32[192,128]{1,0:T(8,128)S(1)}, u32[]{:S(2)}, u32[]{:S(2)}) %collective-permute-start.1) | collective-permute-done | bytes 98336 | tf_op jit(solution)/shard_map/ppermute | solution.py:372
  104.4 0.0 copy-start.8
  104.4 1.5 collective-permute-done.2.g3_ref
  105.8 0.0 copy-start.9
  105.8 0.0 copy-done.7
  105.8 0.0 copy-done.8
  105.8 0.6 copy-done.9
  106.5 2.6 %incoming.1 = f32[8,64,128]{2,1,0:T(8,128)} custom-call(s32[1]{0:T(128)} %bitcast.13.group_ref, f32[8,192,128]{2,1,0:T(8,128)} %get-tuple-element.19.prefix_ref, f32[192,128]{1,0:T(8,128)} %copy-done.7, f32[192,128]{1,0:T(8,128)} %copy-done.8, f32[192,128]{1,0:T(8,128)} %copy-done.9), custom_call_target="tpu_custom_call" | custom-call | tf_op jit(solution)/shard_map/incoming/pallas_call | solution.py:296
  109.1 5.1 %all-to-all-start.2 = ((f32[8,64,128]{2,1,0:T(8,128)}), f32[8,64,128]{2,1,0:T(8,128)S(1)}, u32[]{:S(2)}, u32[]{:S(2)}) async-start(f32[8,64,128]{2,1,0:T(8,128)} %incoming.1), calls=%async_computation.2 | async-start | bytes 524288 | tf_op jit(solution)/shard_map/all_to_all | solution.py:375
  114.2 0.0 copy-start
  114.2 2.2 %copy-done = f32[8,4,128,256]{3,2,1,0:T(8,128)S(1)} copy-done((f32[8,4,128,256]{3,2,1,0:T(8,128)S(1)}, f32[8,4,128,256]{3,2,1,0:T(8,128)}, u32[]{:S(2)}) %copy-start) | copy-done | bytes 4194328
  116.4 0.0 copy-start.1
  116.4 2.2 %copy-done.1 = bf16[8,4,256,256]{3,2,1,0:T(8,128)(2,1)S(1)} copy-done((bf16[8,4,256,256]{3,2,1,0:T(8,128)(2,1)S(1)}, bf16[8,4,256,256]{3,2,1,0:T(8,128)(2,1)}, u32[]{:S(2)}) %copy-start.1) | copy-done | bytes 4194328
  118.6 7.8 %rows.1 = (bf16[8,4,128,256]{3,2,1,0:T(8,128)(2,1)S(1)}, f32[8,4,128,128]{3,2,1,0:T(8,128)S(1)}) custom-call(bf16[8,1040,128]{2,1,0:T(8,128)(2,1)S(1)} %all_to_all.20.x_ref, f32[8,4,128,256]{3,2,1,0:T(8,128)S(1)} %copy-done, bf16[8,4,256,256]{3,2,1,0:T(8,128)(2,1)S(1)} %copy-done.1, f32[8,8,128]{2,1,0:T(8,128)S(1)} %get-tuple-element.15.aux_ref), custom_call_target="tpu_custom_call" | custom-call | flops 2000000000 | bytes 14680064 | tf_op jit(solution)/shard_map/rows/pallas_call | solution.py:240
  126.4 0.0 copy-start.2
  126.4 1.3 copy-done.2
  127.7 0.0 copy-start.3
  127.7 1.3 copy-done.3
  129.1 0.0 all-to-all-done.2
  129.1 0.0 copy-start.4
  129.1 0.7 copy-done.4
  129.8 7.0 %finish.1 = bf16[8,4,128,128]{3,2,1,0:T(8,128)(2,1)} custom-call(bf16[8,4,128,256]{3,2,1,0:T(8,128)(2,1)} %copy-done.2, f32[8,4,128,128]{3,2,1,0:T(8,128)} %copy-done.3, f32[4,128,128]{2,1,0:T(8,128)} %bitcast.33), custom_call_target="tpu_custom_call" | custom-call | tf_op jit(solution)/shard_map/finish/pallas_call | solution.py:321
  136.8 21.4 %all_to_all.22 = bf16[8,4,128,128]{3,2,1,0:T(8,128)(2,1)S(1)} all-to-all(bf16[8,4,128,128]{3,2,1,0:T(8,128)(2,1)} %finish.1), channel_id=1, replica_groups=mesh['ctx'=32,'head'=8] {'head'}, dimensions={0} | all-to-all | bytes 2097152 | tf_op jit(solution)/shard_map/all_to_all | solution.py:386
  158.2 1.6 %copy.11 = bf16[32,128,128]{2,0,1:T(8,128)(2,1)} copy(bf16[32,128,128]{2,1,0:T(8,128)(2,1)S(1)} %bitcast.26) | data formatting | bytes 2097152 | tf_op jit(solution)/shard_map/reshape | solution.py:387
  (3 shorter events, 0.1 us)
Async XLA Ops:
  0.0 1.7 %copy-start.5 = (bf16[128,16,128]{2,1,0:T(8,128)(2,1)S(1)}, bf16[128,16,128]{2,1,0:T(8,128)(2,1)}, u32[]{:S(2)}) copy-start(bf16[128,16,128]{2,1,0:T(8,128)(2,1)} %param.6) | copy-start | bytes 1572868
  0.0 1.9 %copy-start.6 = (bf16[128,16,128]{2,1,0:T(8,128)(2,1)S(1)}, bf16[128,16,128]{2,1,0:T(8,128)(2,1)}, u32[]{:S(2)}) copy-start(bf16[128,16,128]{2,1,0:T(8,128)(2,1)} %param.5) | copy-start | bytes 1572868
  0.0 2.1 %copy-start.10 = (bf16[128,32]{0,1:T(8,128)(2,1)S(1)}, bf16[128,32]{0,1:T(8,128)(2,1)}, u32[]{:S(2)}) copy-start(bf16[128,32]{0,1:T(8,128)(2,1)} %param.8) | copy-start | bytes 24580
  0.0 2.1 %copy-start.11 = (bf16[128,32]{0,1:T(8,128)(2,1)S(1)}, bf16[128,32]{0,1:T(8,128)(2,1)}, u32[]{:S(2)}) copy-start(bf16[128,32]{0,1:T(8,128)(2,1)} %param.9) | copy-start | bytes 24580
  92.4 9.6 %collective-permute-start = (f32[192,128]{1,0:T(8,128)}, f32[192,128]{1,0:T(8,128)S(1)}, u32[]{:S(2)}, u32[]{:S(2)}) collective-permute-start(f32[192,128]{1,0:T(8,128)} %get-tuple-element.20), channel_id=1, source_target_pairs={{0,64},{8,72},{16,80},{24,88},{32,96},{40,104},{48,112},{56,120},{... | collective-permute-start | bytes 294920 | tf_op jit(solution)/shard_map/ppermute | solution.py:372
  95.4 9.0 %collective-permute-start.1 = (f32[192,128]{1,0:T(8,128)}, f32[192,128]{1,0:T(8,128)S(1)}, u32[]{:S(2)}, u32[]{:S(2)}) collective-permute-start(f32[192,128]{1,0:T(8,128)} %get-tuple-element.20), channel_id=1, source_target_pairs={{0,128},{8,136},{16,144},{24,152},{32,160},{40,168},{48,176},{56,1... | collective-permute-start | bytes 294920 | tf_op jit(solution)/shard_map/ppermute | solution.py:372
  99.6 6.2 %collective-permute-start.2 = (f32[192,128]{1,0:T(8,128)}, f32[192,128]{1,0:T(8,128)S(1)}, u32[]{:S(2)}, u32[]{:S(2)}) collective-permute-start(f32[192,128]{1,0:T(8,128)} %get-tuple-element.20), channel_id=1, source_target_pairs={{0,192},{8,200},{16,208},{24,216},{32,224},{40,232},{48,240},{56,2... | collective-permute-start | bytes 294920 | tf_op jit(solution)/shard_map/ppermute | solution.py:372
  102.0 3.9 %copy-start.7 = (f32[192,128]{1,0:T(8,128)}, f32[192,128]{1,0:T(8,128)S(1)}, u32[]{:S(2)}) copy-start(f32[192,128]{1,0:T(8,128)S(1)} %collective-permute-done.g1_ref) | copy-start | bytes 294916
  104.4 1.5 copy-start.8
  105.8 0.7 copy-start.9
  109.1 20.0 %all-to-all-start.2 = ((f32[8,64,128]{2,1,0:T(8,128)}), f32[8,64,128]{2,1,0:T(8,128)S(1)}, u32[]{:S(2)}, u32[]{:S(2)}) async-start(f32[8,64,128]{2,1,0:T(8,128)} %incoming.1), calls=%async_computation.2 | async-start | bytes 524288 | tf_op jit(solution)/shard_map/all_to_all | solution.py:375
  114.2 2.2 %copy-start = (f32[8,4,128,256]{3,2,1,0:T(8,128)S(1)}, f32[8,4,128,256]{3,2,1,0:T(8,128)}, u32[]{:S(2)}) copy-start(f32[8,4,128,256]{3,2,1,0:T(8,128)} %get-tuple-element.13.wu_ref) | copy-start | bytes 12582916
  116.4 2.2 %copy-start.1 = (bf16[8,4,256,256]{3,2,1,0:T(8,128)(2,1)S(1)}, bf16[8,4,256,256]{3,2,1,0:T(8,128)(2,1)}, u32[]{:S(2)}) copy-start(bf16[8,4,256,256]{3,2,1,0:T(8,128)(2,1)} %get-tuple-element.14.ph_ref) | copy-start | bytes 12582916
  126.4 1.3 copy-start.2
  127.7 1.3 copy-start.3
  129.1 0.7 copy-start.4

commit v2 on v0

v2 whole, which is shorter than its diff:
```python
import functools

import jax
import jax.numpy as jnp
from jax import lax
from jax.experimental import pallas as pl
from jax.experimental.pallas import tpu as pltpu
from jax.sharding import PartitionSpec as P

N = 128
CHIPS = 16
SPANS = 4
PAIRS = 4
Q0, G0 = N, 2 * N
KROWS = 2 * N + 16
F32, BF16 = jnp.float32, jnp.bfloat16


def iota(shape, dim):
    return lax.broadcasted_iota(jnp.int32, shape, dim)


def split(x):
    hi = x.astype(BF16)
    return hi, (x - hi.astype(F32)).astype(BF16)


def dot(a, b):
    return jnp.dot(a, b, preferred_element_type=F32)


def dot_nt(a, b):
    return lax.dot_general(a, b, (((1,), (1,)), ((), ())), preferred_element_type=F32)


def dot_tn(a, b):
    return lax.dot_general(a, b, (((0,), (0,)), ((), ())), preferred_element_type=F32)


def dot3(a, b):
    return dot(a[0], b[0]) + dot(a[0], b[1]) + dot(a[1], b[0])


def dot4(a, b):
    wide = jnp.concatenate([a[0], a[1], a[0], a[1]], axis=1)
    return dot(wide, jnp.concatenate([b[0], b[0], b[1], b[1]], axis=0))


def halves(x):
    return x[:, :N], x[:, N:]


def gate_rows(gates):
    upper = (iota((N, N), 0) <= iota((N, N), 1)).astype(F32).astype(BF16)
    return dot(gates, upper)


def gate_columns(gates):
    lower = (iota((N, N), 0) >= iota((N, N), 1)).astype(F32).astype(BF16)
    eye = (iota((N, N), 0) == iota((N, N), 1)).astype(F32).astype(BF16)
    both = dot_nt(jnp.concatenate([lower, eye], axis=0), gates)
    return both[:N], both[N:]


def small_inverses(lower_parts):
    count = len(lower_parts)
    group = iota((16, N), 1) // 16
    rows = []
    for part in lower_parts:
        packed = jnp.zeros((16, N), F32)
        for b in range(8):
            packed = jnp.where(group == b, part[16 * b : 16 * b + 16], packed)
        rows.append(packed)
    packed = jnp.concatenate(rows, axis=0)
    lane = iota((16 * count, N), 1)
    result = (lane % 16 == iota((16 * count, N), 0) % 16).astype(F32).reshape(count, 16, N)
    for j in range(15):
        factor = jnp.take_along_axis(packed, lane // 16 * 16 + j, axis=1).reshape(count, 16, N)
        result = result - factor * result[:, j : j + 1, :]
    return [
        jnp.concatenate([jnp.where(group == b, result[c], 0.0) for b in range(8)], axis=0)
        for c in range(count)
    ]


def merge(inverse, lower_part, size):
    starts = range(size, N, 2 * size)

    def pick(x):
        return jnp.concatenate([x[s : s + size] for s in starts], axis=0)

    half = (N // 2, N)
    row_pair = iota(half, 0) // size
    link = jnp.where(iota(half, 1) // size == 2 * row_pair, pick(lower_part), 0.0)
    hi, lo = split(inverse)
    linked = split(dot3(split(link), (hi, lo)))

    def spread(x):
        zero = jnp.zeros((size, N), BF16)
        pieces = []
        for p in range(len(starts)):
            pieces += [zero, x[p * size : (p + 1) * size]]
        return jnp.concatenate(pieces, axis=0)

    picked = pick(inverse)
    new = picked - dot3((pick(hi), pick(lo)), (spread(linked[0]), spread(linked[1])))
    pieces = []
    for p, s in enumerate(starts):
        pieces += [inverse[s - size : s], new[p * size : (p + 1) * size]]
    return jnp.concatenate(pieces, axis=0)


def params(megabytes):
    return pltpu.CompilerParams(
        dimension_semantics=("arbitrary",), vmem_limit_bytes=megabytes * 2**20
    )


def cost(flops, megabytes):
    return pl.CostEstimate(flops=flops, bytes_accessed=megabytes * 2**20, transcendentals=10**6)


def in_hbm(*arrays):
    return [pltpu.with_memory_space_constraint(x, pltpu.HBM) for x in arrays]


def core_here():
    return lax.axis_index("head") % 2


def group_here():
    return lax.axis_index("ctx") // 4


def spec(*shape):
    return pl.BlockSpec(shape, lambda i: (i,) + (0,) * (len(shape) - 1))


STEP = 4


def solve_kernel(x0_ref, x1_ref, aux_ref, w_ref, tu_ref, m_ref, a_ref):
    first = core_here() == 0
    units = [(x_ref, b, which) for which, x_ref in enumerate((x0_ref, x1_ref)) for b in range(STEP)]
    eye = iota((N, N), 0) == iota((N, N), 1)
    strict = iota((N, N), 0) > iota((N, N), 1)
    lower_parts, scales = [], []
    for x_ref, b, which in units:
        key = x_ref[b, :N]
        gates = x_ref[b, G0 : G0 + 16]
        rows_here = gate_rows(gates)
        cols_here, beta_cols = gate_columns(gates)
        wide = gates.astype(F32)
        brow = jnp.where(first, wide[0:1], wide[1:2])
        bcol = jnp.where(first, beta_cols[:, 0:1], beta_cols[:, 1:2])
        crow = jnp.where(first, rows_here[2:3], rows_here[3:4])
        ccol = jnp.where(first, cols_here[:, 2:3], cols_here[:, 3:4])
        gram = dot_nt(key, key)
        diagonal = jnp.where(eye, gram, 0.0)
        norm_row = lax.rsqrt(jnp.sum(diagonal, axis=0, keepdims=True) + 1e-06)
        norm_col = lax.rsqrt(jnp.sum(diagonal, axis=1, keepdims=True) + 1e-06)
        decay = jnp.exp(jnp.minimum(ccol - crow, 0.0))
        scaled = gram * (norm_col * bcol) * norm_row * decay
        lower_parts.append(jnp.where(strict, scaled, 0.0))
        last = crow[:, N - 1 : N]
        scales.append((
            brow * jnp.exp(crow) * norm_row,
            brow,
            norm_col * jnp.exp(last - ccol),
            jnp.exp(last),
        ))
        aux_ref[b, which] = jnp.concatenate([crow, norm_row, jnp.zeros((6, N), F32)], axis=0)
    inverses = small_inverses(lower_parts)
    for size in (16, 32, 64):
        inverses = [merge(t, g, size) for t, g in zip(inverses, lower_parts)]
    for inverse, (for_w, for_u, for_state, last), (x_ref, b, which) in zip(inverses, scales, units):
        key = x_ref[b, :N]
        hi, lo = split(inverse * for_w)
        w = dot(hi, key) + dot(lo, key)
        tu = inverse * for_u
        tu_ref[b, which] = jnp.concatenate(split(tu), axis=1)
        w_ref[b, which] = w
        hi, lo = split(jnp.concatenate([w, tu], axis=1) * for_state)
        both = dot_tn(key, hi) + dot_tn(key, lo)
        a_ref[b, which] = jnp.concatenate(split(jnp.where(eye, last, 0.0) - both[:, :N]), axis=1)
        m_ref[b, which] = jnp.concatenate(split(both[:, N:]), axis=1)


def solve(x0, x1):
    return pl.pallas_call(
        solve_kernel,
        grid=(CHIPS // STEP,),
        in_specs=[spec(STEP, KROWS, N)] * 2,
        out_specs=[spec(STEP, 2, 8, N), spec(STEP, 2, N, N)] + [spec(STEP, 2, N, 2 * N)] * 3,
        out_shape=[
            pltpu.HBM((CHIPS, 2, 8, N), F32),
            pltpu.HBM((CHIPS, 2, N, N), F32),
        ]
        + [pltpu.HBM((CHIPS, 2, N, 2 * N), BF16)] * 3,
        compiler_params=params(24),
        cost_estimate=cost(16 * 10**9, 20),
        name="solve",
    )(x0, x1)


def later(a, offset, parts):
    moved = dot4(a, parts)
    return jnp.concatenate([moved[:, :N], moved[:, N:] + offset], axis=1)


def unit_pair():
    return jnp.where(iota((N, 2 * N), 0) == iota((N, 2 * N), 1), 1.0, 0.0)


def chain_kernel(m_ref, a_ref, v_ref, ph_ref, start_ref, total_ref, state):
    step = pl.program_id(0)

    @pl.when(step == 0)
    def _():
        for s in range(SPANS):
            state[s] = unit_pair()

    def advance(order):
        for place, which in enumerate(order):
            for s in range(SPANS):
                value = v_ref[s, 0, place]
                hi, lo = halves(m_ref[s, 0, which])
                offset = dot(hi, value) + dot(lo, value)
                parts = split(state[s])
                ph_ref[s, 0, which] = jnp.concatenate(parts, axis=0)
                state[s] = later(halves(a_ref[s, 0, which]), offset, parts)

    @pl.when(core_here() == 0)
    def _():
        advance((0, 1))

    @pl.when(core_here() != 0)
    def _():
        advance((1, 0))

    @pl.when(step == PAIRS - 1)
    def _():
        running = state[0]
        start_ref[0] = unit_pair()
        for s in range(1, SPANS):
            start_ref[s] = running
            running = later(split(state[s, :, :N]), state[s, :, N:], split(running))
        total_ref[...] = running


def chain(m, a, v):
    def of_pair(*shape):
        return pl.BlockSpec((SPANS, 1) + shape, lambda i: (0, i) + (0,) * len(shape))

    m, a = (x.reshape(SPANS, PAIRS, 2, N, 2 * N) for x in (m, a))
    return pl.pallas_call(
        chain_kernel,
        grid=(PAIRS,),
        in_specs=[of_pair(2, N, 2 * N)] * 2 + [of_pair(2, N, N)],
        out_specs=[
            of_pair(2, 2 * N, 2 * N),
            pl.BlockSpec((SPANS, N, 2 * N), lambda i: (0, 0, 0)),
            pl.BlockSpec((N, 2 * N), lambda i: (0, 0)),
        ],
        out_shape=[
            jax.ShapeDtypeStruct((SPANS, PAIRS, 2, 2 * N, 2 * N), BF16),
            jax.ShapeDtypeStruct((SPANS, N, 2 * N), F32),
            jax.ShapeDtypeStruct((N, 2 * N), F32),
        ],
        scratch_shapes=[pltpu.VMEM((SPANS, N, 2 * N), F32)],
        compiler_params=params(16),
        cost_estimate=cost(4 * 10**9, 10),
        name="chain",
    )(*in_hbm(m, a), v.reshape(SPANS, PAIRS, 2, N, N))


ROWSTEP = 4


def rows_kernel(which, x_ref, v_ref, aux_ref, w_ref, tu_ref, ph_ref, r_ref, o_ref):
    core = core_here()
    first = core == 0
    place = core if which == 0 else 1 - core
    inclusive = iota((N, N), 0) >= iota((N, N), 1)
    for b in range(ROWSTEP):
        key, query, value = x_ref[b, :N], x_ref[b, Q0 : Q0 + N], v_ref[b, place]
        cols_here, _ = gate_columns(x_ref[b, G0 : G0 + 16])
        ccol = jnp.where(first, cols_here[:, 2:3], cols_here[:, 3:4])
        wide = query.astype(F32)
        norm = lax.rsqrt(jnp.sum(wide * wide, axis=1, keepdims=True) + 1e-06) * N ** (-0.5)
        decay = jnp.exp(jnp.minimum(ccol - aux_ref[b, 0:1], 0.0))
        scores = dot_nt(query, key) * norm * aux_ref[b, 1:2] * decay
        scores = jnp.where(inclusive, scores, 0.0)
        hi, lo = halves(tu_ref[b])
        u = dot(hi, value) + dot(lo, value)
        inner = dot4(split(scores), split(jnp.concatenate([w_ref[b], u], axis=1)))
        reach = split(wide * (norm * jnp.exp(ccol)) - inner[:, :N])
        both = dot4(reach, (ph_ref[b, :N], ph_ref[b, N:]))
        r_ref[b] = jnp.concatenate(split(both[:, :N]), axis=1)
        o_ref[b] = both[:, N:] + inner[:, N:]


def rows(which, x, v, aux, w, tu, ph):
    def one_of(*shape):
        return pl.BlockSpec((ROWSTEP, None) + shape, lambda i: (i, which) + (0,) * len(shape))

    return pl.pallas_call(
        functools.partial(rows_kernel, which),
        grid=(CHIPS // ROWSTEP,),
        in_specs=[
            spec(ROWSTEP, KROWS, N),
            spec(ROWSTEP, 2, N, N),
            one_of(8, N),
            one_of(N, N),
            one_of(N, 2 * N),
            one_of(2 * N, 2 * N),
        ],
        out_specs=[spec(ROWSTEP, N, 2 * N), spec(ROWSTEP, N, N)],
        out_shape=[
            jax.ShapeDtypeStruct((CHIPS, N, 2 * N), BF16),
            jax.ShapeDtypeStruct((CHIPS, N, N), F32),
        ],
        compiler_params=params(16),
        cost_estimate=cost(5 * 10**9, 8),
        name="rows",
    )(x, v.reshape(CHIPS, 2, N, N), aux, w, tu, ph.reshape(CHIPS, 2, 2 * N, 2 * N))


def first_join_kernel(got_ref, own_ref, before_ref, run_ref):
    before = jnp.where(group_here() >= 1, got_ref[...], unit_pair())
    own = own_ref[...]
    before_ref[...] = before
    run_ref[...] = later(split(own[:, :N]), own[:, N:], split(before))


def second_join_kernel(got_ref, before_ref, run_ref, longer_ref, offset_ref):
    got = split(jnp.where(group_here() >= 2, got_ref[...], unit_pair()))
    run, before = run_ref[...], before_ref[...]
    offset_ref[...] = dot4(split(run[:, :N]), (got[0][:, N:], got[1][:, N:])) + run[:, N:]
    longer_ref[...] = later(split(before[:, :N]), before[:, N:], got)


def joined(kernel, outs, *args):
    vmem = pl.BlockSpec(memory_space=pltpu.VMEM)
    return pl.pallas_call(
        kernel,
        in_specs=[vmem] * len(args),
        out_shape=[jax.ShapeDtypeStruct((N, width), F32) for width in outs],
        compiler_params=pltpu.CompilerParams(vmem_limit_bytes=8 * 2**20),
    )(*args)


def finish_kernel(got_ref, longer_ref, start_ref, r0, o0, r1, o1, out_ref, state):
    step = pl.program_id(0)

    @pl.when(step == 0)
    def _():
        offset = jnp.where(group_here() >= 4, got_ref[...], 0.0)
        before = longer_ref[...]
        first = dot4(split(before[:, :N]), split(offset)) + before[:, N:]
        parts = split(first)
        state[0] = jnp.concatenate(parts, axis=0)
        for s in range(1, SPANS):
            pair = start_ref[s]
            state[s] = jnp.concatenate(
                split(dot4(split(pair[:, :N]), parts) + pair[:, N:]), axis=0
            )

    rhs = state[step]
    core = core_here()
    for b in range(PAIRS):
        for place, r_ref, o_ref in ((core, r0, o0), (1 - core, r1, o1)):
            out = dot4(halves(r_ref[b]), (rhs[:N], rhs[N:])) + o_ref[b]
            out_ref[b, place] = out.astype(BF16)


def finish(got, longer, start, r0, o0, r1, o1):
    return pl.pallas_call(
        finish_kernel,
        grid=(SPANS,),
        in_specs=[
            pl.BlockSpec((N, N), lambda i: (0, 0)),
            pl.BlockSpec((N, 2 * N), lambda i: (0, 0)),
            pl.BlockSpec((SPANS, N, 2 * N), lambda i: (0, 0, 0)),
        ]
        + [spec(PAIRS, N, 2 * N), spec(PAIRS, N, N)] * 2,
        out_specs=spec(PAIRS, 2, N, N),
        out_shape=jax.ShapeDtypeStruct((CHIPS, 2, N, N), BF16),
        scratch_shapes=[pltpu.VMEM((SPANS, 2 * N, N), BF16)],
        compiler_params=params(16),
        cost_estimate=cost(10**9, 5),
        name="finish",
    )(got, longer, start, r0, o0, r1, o1)


PACKSTEP = 32


def pack_kernel(k_ref, q_ref, beta_ref, gate_ref, out_ref, wide):
    step = pl.program_id(0)
    for start, ref in ((0, k_ref), (Q0, q_ref)):
        wide[start // N] = ref[...].astype(F32).reshape(16 * PACKSTEP, N)
        row = pl.multiple_of(start + step * PACKSTEP, PACKSTEP)
        for h in range(16):
            rows = wide[start // N, pl.ds(h, PACKSTEP, stride=16), :]
            out_ref[h, pl.ds(row, PACKSTEP), :] = rows.astype(BF16)

    @pl.when(step == 0)
    def _():
        beta, gate = beta_ref[...].astype(F32), gate_ref[...].astype(F32)
        for h in range(16):
            pair = slice(2 * h, 2 * h + 2)
            tail = jnp.concatenate([beta[pair], gate[pair], jnp.zeros((12, N), F32)], axis=0)
            out_ref[h, G0:] = tail.astype(BF16)


def pack(key_rows, query_rows, beta_rows, log_gate):
    return pl.pallas_call(
        pack_kernel,
        grid=(N // PACKSTEP,),
        in_specs=[spec(PACKSTEP, 16, N)] * 2 + [pl.BlockSpec((32, N), lambda i: (0, 0))] * 2,
        out_specs=pl.BlockSpec((CHIPS, KROWS, N), lambda i: (0, 0, 0)),
        out_shape=jax.ShapeDtypeStruct((CHIPS, KROWS, N), BF16),
        scratch_shapes=[pltpu.VMEM((2, 16 * PACKSTEP, N), F32)],
        compiler_params=params(60),
        name="pack",
    )(key_rows, query_rows, beta_rows.T, log_gate.T)


EVERY = [list(range(32 * g, 32 * g + 32)) for g in range(8)]
ALIKE = [list(range(32 * g + core, 32 * g + 32, 2)) for g in range(8) for core in range(2)]


def exchange(x, groups):
    return lax.all_to_all(x, ("ctx", "head"), 0, 0, tiled=True, axis_index_groups=groups)


def onward(x, groups):
    ring = [(i, (i + 4 * groups) % 32) for i in range(32)]
    return lax.ppermute(x, "ctx", ring)


def other_core(x):
    return lax.ppermute(x, "head", [(i, i ^ 1) for i in range(8)])


def local(query_rows, key_rows, value_rows, beta_rows, log_gate):
    x0 = exchange(pack(key_rows, query_rows, beta_rows, log_gate), ALIKE)
    values, x0 = lax.optimization_barrier((value_rows.transpose(1, 0, 2), x0))
    x1 = other_core(x0)
    v = exchange(values, EVERY)
    aux, w, tu, m, a = solve(x0, x1)
    ph, start, total = chain(m, a, v)
    before, run = joined(first_join_kernel, (2 * N, 2 * N), onward(total, 1), total)
    longer, offset = joined(second_join_kernel, (2 * N, N), onward(run, 2), before, run)
    got = onward(offset, 4)
    r0, o0 = rows(0, x0, v, aux, w, tu, ph)
    r1, o1 = rows(1, x1, v, aux, w, tu, ph)
    out = finish(got, longer, start, r0, o0, r1, o1)
    return exchange(out.reshape(2 * CHIPS, N, N), EVERY).transpose(1, 0, 2)


def solution(mesh):
    placed = (
        P(("ctx", "head"), None, None),
        P(("ctx", "head"), None, None),
        P(("ctx", "head"), None, None),
        P(("ctx", "head"), None),
        P(("ctx", "head"), None),
    )
    return jax.shard_map(
        local, mesh=mesh, in_specs=placed, out_specs=P(("ctx", "head"), None, None), check_vma=False
    )
```

time: 1150 us -> 118 us (0.10)
  other arithmetic: 659 us -> 0 us
  waiting for transfers between devices: 212 us -> 23.9 us
  matrix products: 146 us -> 0 us
  local copies, waits for them, and re-layouts: 68.1 us -> 3.04 us
  Pallas kernels: 0 us -> 45.8 us
  between operations: 13.6 us -> 0.14 us
    another operation x64 -> x0, other arithmetic: 637 us -> none  [the longest x48 634 us: advance(): jax.scipy.linalg.solve_triangular(mat, rhs_part, lower=True, unit_diagona...]
    all_gather x2 -> x0, waiting for transfers between devices: 178 us -> none  [entering(): pieces = jax.tree.map(lambda part: lax.all_gather(part, axis), value)]
    dot_general x103 -> x0, matrix products: 124 us -> none  [the longest x31 48.4 us: compose(): jnp.einsum('hij,hjk->hik', earlier[1], later[0], precision=highest)]
    pallas_call x0 -> x8, Pallas kernels: none -> 45.8 us  [the longest x1 18.6 us: solve(): pl.pallas_call(solve_kernel, grid=(CHIPS // STEP,), in_specs=[spec(STEP,...]
    dynamic_slice x62 -> x0, local copies, waits for them, and re-layouts: 34.1 us -> none  [step(): longer = join(subtotal, jax.tree.map(lambda part: part[position], pieces))]
    another operation x16 -> x0, matrix products: 21.3 us -> none  [advance(): jax.scipy.linalg.solve_triangular(mat, rhs_part, lower=True, unit_diagona...]
    all_to_all x4 -> x2, waiting for transfers between devices: 33.2 us -> 14.7 us  [exchange(): lax.all_to_all(x, ('ctx', 'head'), 0, 0, tiled=True, axis_index_groups=gr...]
    slice x8 -> x0, other arithmetic: 14.4 us -> none  [advance(): right_side[..., :split_at]]
  transfers between devices with their start and end apart: 6 -> 6, of which waited for: 6 -> 3; matrix products, arithmetic and copies ran while one was open for 1% -> 1% of each run, Pallas kernels for 0% -> 29%
where the time goes in v2:
time: 118 us
  Pallas kernels  45.8 us (39%)
  blocking collectives  24.3 us (21%)
  waiting for transfers between devices  23.9 us (20%)
  starting transfers between devices  20.4 us (17%)
  local copies, waits for them, and re-layouts  3.04 us (3%)
    all_to_all x1, blocking collectives, exchange(): lax.all_to_all(x, ('ctx', 'head'), 0, 0, tiled=True, axis_index_groups=gr...  24.3 us
    pallas_call x1, Pallas kernels, solve(): pl.pallas_call(solve_kernel, grid=(CHIPS // STEP,), in_specs=[spec(STEP,...  18.6 us
    pallas_call x2, Pallas kernels, rows(): pl.pallas_call(functools.partial(rows_kernel, which), grid=(CHIPS // ROWS...  15.2 us
    all_to_all x2, waiting for transfers between devices, exchange(): lax.all_to_all(x, ('ctx', 'head'), 0, 0, tiled=True, axis_index_groups=gr...  14.7 us
    all_to_all x2, starting transfers between devices, exchange(): lax.all_to_all(x, ('ctx', 'head'), 0, 0, tiled=True, axis_index_groups=gr...  11.3 us
    ppermute x3, waiting for transfers between devices, onward(): return lax.ppermute(x, 'ctx', ring)  9.18 us
    ppermute x3, starting transfers between devices, onward(): return lax.ppermute(x, 'ctx', ring)  5.68 us
    pallas_call x1, Pallas kernels, chain(): pl.pallas_call(chain_kernel, grid=(PAIRS,), in_specs=[of_pair(2, N, 2 * N...  5.67 us
  transfers between devices with their start and end apart: 6, of which 3 were waited for; matrix products, arithmetic and copies ran while one was open for 1% of the time, Pallas kernels for 29%

profile of v2, /device:TPU:1, one launch (start us, length us, event | category | flops | bytes accessed | tf_op | source)
XLA Modules:
  0.0 117.5 jit_solution(11935814421053525112)
XLA Ops:
  0.0 0.0 copy-start.3
  0.0 3.7 %pack.1 = bf16[16,272,128]{2,1,0:T(8,128)(2,1)} custom-call(bf16[128,16,128]{2,1,0:T(8,128)(2,1)} %k_ref.1, bf16[128,16,128]{2,1,0:T(8,128)(2,1)} %q_ref.1, bf16[32,128]{1,0:T(8,128)(2,1)} %bitcast.20, bf16[32,128]{1,0:T(8,128)(2,1)} %bitcast.21), custom_call_target="tpu_custom_call" | custom-call | tf_op jit(solution)/shard_map/pack/pallas_call | solution.py:418
  3.7 7.6 %all-to-all-start = ((bf16[16,272,128]{2,1,0:T(8,128)(2,1)}), bf16[16,272,128]{2,1,0:T(8,128)(2,1)S(1)}, u32[]{:S(2)}, u32[]{:S(2)}) async-start(bf16[16,272,128]{2,1,0:T(8,128)(2,1)} %pack.1), calls=%async_computation | async-start | bytes 2228224 | tf_op jit(solution)/shard_map/all_to_all | solution.py:435
  11.3 0.0 copy-done.3
  11.3 1.4 %copy.12 = bf16[128,32,128]{2,0,1:T(8,128)(2,1)} copy(bf16[128,32,128]{2,1,0:T(8,128)(2,1)S(1)} %copy-done.3) | data formatting | bytes 2097152 | tf_op args[2]
  12.6 14.7 %all-to-all-done.x0_ref.x_ref = bf16[16,272,128]{2,1,0:T(8,128)(2,1)S(1)} async-done(((bf16[16,272,128]{2,1,0:T(8,128)(2,1)}), bf16[16,272,128]{2,1,0:T(8,128)(2,1)S(1)}, u32[]{:S(2)}, u32[]{:S(2)}) %all-to-all-start) | async-done | bytes 1114144 | tf_op jit(solution)/shard_map/all_to_all | solution.py:435
  27.3 3.4 %collective-permute-start = (bf16[16,272,128]{2,1,0:T(8,128)(2,1)S(1)}, bf16[16,272,128]{2,1,0:T(8,128)(2,1)S(1)}, u32[]{:S(2)}, u32[]{:S(2)}) collective-permute-start(bf16[16,272,128]{2,1,0:T(8,128)(2,1)S(1)} %all-to-all-done.x0_ref.x_ref), channel_id=1, source_target_pairs={{0,1},{1,0},{2,3},{3,2},{4,5},{5,4},{6,7},{7,6},{8,9},{9,8},{10,11... | collective-permute-start | bytes 3342344 | tf_op jit(solution)/shard_map/ppermute | solution.py:444
  30.7 3.7 %all-to-all-start.1 = ((bf16[32,128,128]{2,1,0:T(8,128)(2,1)}), bf16[32,128,128]{2,1,0:T(8,128)(2,1)S(1)}, u32[]{:S(2)}, u32[]{:S(2)}) async-start(bf16[32,128,128]{2,1,0:T(8,128)(2,1)} %bitcast.18), calls=%async_computation.1 | async-start | bytes 2097152 | tf_op jit(solution)/shard_map/all_to_all | solution.py:435
  34.4 0.0 collective-permute-done.x1_ref.x_ref
  34.5 18.6 %solve.1 = (f32[16,2,8,128]{3,2,1,0:T(8,128)}, f32[16,2,128,128]{3,2,1,0:T(8,128)}, bf16[16,2,128,256]{3,2,1,0:T(8,128)(2,1)}, bf16[16,2,128,256]{3,2,1,0:T(8,128)(2,1)}, bf16[16,2,128,256]{3,2,1,0:T(8,128)(2,1)}) custom-call(bf16[16,272,128]{2,1,0:T(8,128)(2,1)S(1)} %all-to-all-done.x0_ref.x_ref, bf16[16,272,128]{2,1,0:T(8,128)(2,1)S(1)} %collective-permute-done.x1_ref.x_ref), custom_call_target="tpu_custom_call" | custom-call | flops 16000000000 | bytes 20971520 | tf_op jit(solution)/shard_map/solve/pallas_call | solution.py:190
  53.1 0.0 all-to-all-done.1
  53.1 0.0 copy-start
  53.1 0.0 copy-start.1
  53.1 0.0 copy-start.2
  53.1 5.7 %chain.1 = (bf16[4,4,2,256,256]{4,3,2,1,0:T(8,128)(2,1)S(1)}, f32[4,128,256]{2,1,0:T(8,128)S(1)}, f32[128,256]{1,0:T(8,128)S(1)}) custom-call(bf16[4,4,2,128,256]{4,3,2,1,0:T(8,128)(2,1)} %bitcast.22, bf16[4,4,2,128,256]{4,3,2,1,0:T(8,128)(2,1)} %bitcast.23, bf16[4,4,2,128,128]{4,3,2,1,0:T(8,128)(2,1)S(1)} %bitcast.13), custom_call_target="tpu_custom_call" | custom-call | flops 4000000000 | bytes 10485760 | tf_op jit(solution)/shard_map/chain/pallas_call | solution.py:256
  58.8 1.7 %collective-permute-start.1 = (f32[128,256]{1,0:T(8,128)S(1)}, f32[128,256]{1,0:T(8,128)S(1)}, u32[]{:S(2)}, u32[]{:S(2)}) collective-permute-start(f32[128,256]{1,0:T(8,128)S(1)} %get-tuple-element.27.own_ref), channel_id=1, source_target_pairs={{0,32},{8,40},{16,48},{24,56},{32,64},{40,72},{48,80},{56,88},{64,... | collective-permute-start | bytes 393224 | tf_op jit(solution)/shard_map/ppermute | solution.py:440
  60.5 7.7 %collective-permute-done.1.got_ref = f32[128,256]{1,0:T(8,128)S(1)} collective-permute-done((f32[128,256]{1,0:T(8,128)S(1)}, f32[128,256]{1,0:T(8,128)S(1)}, u32[]{:S(2)}, u32[]{:S(2)}) %collective-permute-start.1) | collective-permute-done | bytes 131104 | tf_op jit(solution)/shard_map/ppermute | solution.py:440
  68.2 0.2 shard_map.55
  68.4 0.1 collective-permute-start.2
  68.5 0.0 copy-done
  68.5 0.0 copy-done.1
  68.5 0.0 copy-done.2
  68.5 7.6 %rows.2 = (bf16[16,128,256]{2,1,0:T(8,128)(2,1)S(1)}, f32[16,128,128]{2,1,0:T(8,128)S(1)}) custom-call(bf16[16,272,128]{2,1,0:T(8,128)(2,1)S(1)} %all-to-all-done.x0_ref.x_ref, bf16[16,2,128,128]{3,2,1,0:T(8,128)(2,1)S(1)} %bitcast.14, f32[16,2,8,128]{3,2,1,0:T(8,128)S(1)} %copy-done.2, f32[16,2,128,128]{3,2,1,0:T(8,128)S(1)} %copy-done, ...), custom_call_target="tpu_custom_call" | custom-call | flops 5000000000 | bytes 8388608 | tf_op jit(solution)/shard_map/rows/pallas_call | solution.py:307
  76.1 1.5 %collective-permute-done.2.got_ref = f32[128,256]{1,0:T(8,128)S(1)} collective-permute-done((f32[128,256]{1,0:T(8,128)S(1)}, f32[128,256]{1,0:T(8,128)S(1)}, u32[]{:S(2)}, u32[]{:S(2)}) %collective-permute-start.2) | collective-permute-done | bytes 131104 | tf_op jit(solution)/shard_map/ppermute | solution.py:440
  77.7 0.2 shard_map.56
  77.9 3.9 %collective-permute-start.3 = (f32[128,128]{1,0:T(8,128)S(1)}, f32[128,128]{1,0:T(8,128)S(1)}, u32[]{:S(2)}, u32[]{:S(2)}) collective-permute-start(f32[128,128]{1,0:T(8,128)S(1)} %get-tuple-element.30), channel_id=1, source_target_pairs={{0,128},{8,136},{16,144},{24,152},{32,160},{40,168},{48,176},{56,1... | collective-permute-start | bytes 196616 | tf_op jit(solution)/shard_map/ppermute | solution.py:440
  81.8 7.6 %rows.3 = (bf16[16,128,256]{2,1,0:T(8,128)(2,1)S(1)}, f32[16,128,128]{2,1,0:T(8,128)S(1)}) custom-call(bf16[16,272,128]{2,1,0:T(8,128)(2,1)S(1)} %collective-permute-done.x1_ref.x_ref, bf16[16,2,128,128]{3,2,1,0:T(8,128)(2,1)S(1)} %bitcast.15, f32[16,2,8,128]{3,2,1,0:T(8,128)S(1)} %copy-done.2, f32[16,2,128,128]{3,2,1,0:T(8,128)S(1)} %copy-done, ...), custom_call_target="tpu_custom_call" | custom-call | flops 5000000000 | bytes 8388608 | tf_op jit(solution)/shard_map/rows/pallas_call | solution.py:307
  89.4 0.0 collective-permute-done.3.got_ref
  89.4 2.2 %finish.1 = bf16[16,2,128,128]{3,2,1,0:T(8,128)(2,1)S(1)} custom-call(f32[128,128]{1,0:T(8,128)S(1)} %collective-permute-done.3.got_ref, f32[128,256]{1,0:T(8,128)S(1)} %get-tuple-element.31.longer_ref, f32[4,128,256]{2,1,0:T(8,128)S(1)} %get-tuple-element.32.start_ref, bf16[16,128,256]{2,1,0:T(8,128)(2,1)S(1)} %get-tuple-element.37.r0, ...), custom_call_target="tpu_custom_call" | custom-call | flops 1000000000 | bytes 5242880 | tf_op jit(solution)/shard_map/finish/pallas_call | solution.py:378
  91.6 24.3 %all_to_all.15 = bf16[32,128,128]{2,1,0:T(8,128)(2,1)S(1)} all-to-all(bf16[32,128,128]{2,1,0:T(8,128)(2,1)S(1)} %bitcast.12), channel_id=1, replica_groups={{0,1,2,3,4,5,6,7,8,9,10,11,12,13,14,15,16,17,18,19,20,21,22,23,24,25,26..., dimensions={0} | all-to-all | bytes 2097152 | tf_op jit(solution)/shard_map/all_to_all | solution.py:435
  115.9 1.6 %copy.10 = bf16[128,32,128]{2,1,0:T(8,128)(2,1)} copy(bf16[128,32,128]{2,0,1:T(8,128)(2,1)S(1)} %bitcast.19) | data formatting | bytes 2097152 | tf_op jit(solution)/shard_map/transpose | solution.py:460
Async XLA Ops:
  0.0 11.3 %copy-start.3 = (bf16[128,32,128]{2,1,0:T(8,128)(2,1)S(1)}, bf16[128,32,128]{2,1,0:T(8,128)(2,1)}, u32[]{:S(2)}) copy-start(bf16[128,32,128]{2,1,0:T(8,128)(2,1)} %param.7) | copy-start | bytes 3145732
  3.7 23.7 %all-to-all-start = ((bf16[16,272,128]{2,1,0:T(8,128)(2,1)}), bf16[16,272,128]{2,1,0:T(8,128)(2,1)S(1)}, u32[]{:S(2)}, u32[]{:S(2)}) async-start(bf16[16,272,128]{2,1,0:T(8,128)(2,1)} %pack.1), calls=%async_computation | async-start | bytes 2228224 | tf_op jit(solution)/shard_map/all_to_all | solution.py:435
  27.3 7.1 %collective-permute-start = (bf16[16,272,128]{2,1,0:T(8,128)(2,1)S(1)}, bf16[16,272,128]{2,1,0:T(8,128)(2,1)S(1)}, u32[]{:S(2)}, u32[]{:S(2)}) collective-permute-start(bf16[16,272,128]{2,1,0:T(8,128)(2,1)S(1)} %all-to-all-done.x0_ref.x_ref), channel_id=1, source_target_pairs={{0,1},{1,0},{2,3},{3,2},{4,5},{5,4},{6,7},{7,6},{8,9},{9,8},{10,11... | collective-permute-start | bytes 3342344 | tf_op jit(solution)/shard_map/ppermute | solution.py:444
  30.7 22.4 %all-to-all-start.1 = ((bf16[32,128,128]{2,1,0:T(8,128)(2,1)}), bf16[32,128,128]{2,1,0:T(8,128)(2,1)S(1)}, u32[]{:S(2)}, u32[]{:S(2)}) async-start(bf16[32,128,128]{2,1,0:T(8,128)(2,1)} %bitcast.18), calls=%async_computation.1 | async-start | bytes 2097152 | tf_op jit(solution)/shard_map/all_to_all | solution.py:435
  53.1 15.4 %copy-start = (f32[16,2,128,128]{3,2,1,0:T(8,128)S(1)}, f32[16,2,128,128]{3,2,1,0:T(8,128)}, u32[]{:S(2)}) copy-start(f32[16,2,128,128]{3,2,1,0:T(8,128)} %get-tuple-element.34.w_ref) | copy-start | bytes 6291460
  53.1 15.4 %copy-start.1 = (bf16[16,2,128,256]{3,2,1,0:T(8,128)(2,1)S(1)}, bf16[16,2,128,256]{3,2,1,0:T(8,128)(2,1)}, u32[]{:S(2)}) copy-start(bf16[16,2,128,256]{3,2,1,0:T(8,128)(2,1)} %get-tuple-element.35.tu_ref) | copy-start | bytes 6291460
  53.1 15.4 %copy-start.2 = (f32[16,2,8,128]{3,2,1,0:T(8,128)S(1)}, f32[16,2,8,128]{3,2,1,0:T(8,128)}, u32[]{:S(2)}) copy-start(f32[16,2,8,128]{3,2,1,0:T(8,128)} %get-tuple-element.33.aux_ref) | copy-start | bytes 393220
  58.8 9.4 %collective-permute-start.1 = (f32[128,256]{1,0:T(8,128)S(1)}, f32[128,256]{1,0:T(8,128)S(1)}, u32[]{:S(2)}, u32[]{:S(2)}) collective-permute-start(f32[128,256]{1,0:T(8,128)S(1)} %get-tuple-element.27.own_ref), channel_id=1, source_target_pairs={{0,32},{8,40},{16,48},{24,56},{32,64},{40,72},{48,80},{56,88},{64,... | collective-permute-start | bytes 393224 | tf_op jit(solution)/shard_map/ppermute | solution.py:440
  68.4 9.3 %collective-permute-start.2 = (f32[128,256]{1,0:T(8,128)S(1)}, f32[128,256]{1,0:T(8,128)S(1)}, u32[]{:S(2)}, u32[]{:S(2)}) collective-permute-start(f32[128,256]{1,0:T(8,128)S(1)} %get-tuple-element.28.run_ref), channel_id=1, source_target_pairs={{0,64},{8,72},{16,80},{24,88},{32,96},{40,104},{48,112},{56,120},{... | collective-permute-start | bytes 393224 | tf_op jit(solution)/shard_map/ppermute | solution.py:440
  77.9 11.5 %collective-permute-start.3 = (f32[128,128]{1,0:T(8,128)S(1)}, f32[128,128]{1,0:T(8,128)S(1)}, u32[]{:S(2)}, u32[]{:S(2)}) collective-permute-start(f32[128,128]{1,0:T(8,128)S(1)} %get-tuple-element.30), channel_id=1, source_target_pairs={{0,128},{8,136},{16,144},{24,152},{32,160},{40,168},{48,176},{56,1... | collective-permute-start | bytes 196616 | tf_op jit(solution)/shard_map/ppermute | solution.py:440

commit v3 on v2

--- a/solution.py
+++ b/solution.py
@@ -37,8 +37,18 @@
     return lax.dot_general(a, b, (((0,), (0,)), ((), ())), preferred_element_type=F32)
 
 
+def dot_stacked(stacked, b):
+    rows = stacked.shape[0] // 2
+    both = dot(stacked, b)
+    return both[:rows] + both[rows:]
+
+
+def stack(parts):
+    return jnp.concatenate(parts, axis=0)
+
+
 def dot3(a, b):
-    return dot(a[0], b[0]) + dot(a[0], b[1]) + dot(a[1], b[0])
+    return dot_stacked(stack(a), b[0]) + dot(a[0], b[1])
 
 
 def dot4(a, b):
@@ -83,17 +93,15 @@
     ]
 
 
-def merge(inverse, lower_part, size):
+def merge(parts, lower_part, size):
     starts = range(size, N, 2 * size)
 
     def pick(x):
         return jnp.concatenate([x[s : s + size] for s in starts], axis=0)
 
     half = (N // 2, N)
-    row_pair = iota(half, 0) // size
-    link = jnp.where(iota(half, 1) // size == 2 * row_pair, pick(lower_part), 0.0)
-    hi, lo = split(inverse)
-    linked = split(dot3(split(link), (hi, lo)))
+    link = jnp.where(iota(half, 1) // size == 2 * (iota(half, 0) // size), pick(lower_part), 0.0)
+    linked = split(dot3(split(link), parts[1:]))
 
     def spread(x):
         zero = jnp.zeros((size, N), BF16)
@@ -102,12 +110,16 @@
             pieces += [zero, x[p * size : (p + 1) * size]]
         return jnp.concatenate(pieces, axis=0)
 
-    picked = pick(inverse)
-    new = picked - dot3((pick(hi), pick(lo)), (spread(linked[0]), spread(linked[1])))
-    pieces = []
-    for p, s in enumerate(starts):
-        pieces += [inverse[s - size : s], new[p * size : (p + 1) * size]]
-    return jnp.concatenate(pieces, axis=0)
+    picked = [pick(x) for x in parts]
+    new = picked[0] - dot3(picked[1:], (spread(linked[0]), spread(linked[1])))
+
+    def renew(old, fresh):
+        pieces = []
+        for p, s in enumerate(starts):
+            pieces += [old[s - size : s], fresh[p * size : (p + 1) * size]]
+        return jnp.concatenate(pieces, axis=0)
+
+    return [renew(old, fresh) for old, fresh in zip(parts, (new,) + split(new))]
 
 
 def params(megabytes):
@@ -136,7 +148,7 @@
     return pl.BlockSpec(shape, lambda i: (i,) + (0,) * (len(shape) - 1))
 
 
-STEP = 4
+STEP = 16
 
 
 def solve_kernel(x0_ref, x1_ref, aux_ref, w_ref, tu_ref, m_ref, a_ref):
@@ -170,20 +182,20 @@
             jnp.exp(last),
         ))
         aux_ref[b, which] = jnp.concatenate([crow, norm_row, jnp.zeros((6, N), F32)], axis=0)
-    inverses = small_inverses(lower_parts)
+    inverses = [(t,) + split(t) for t in small_inverses(lower_parts)]
     for size in (16, 32, 64):
         inverses = [merge(t, g, size) for t, g in zip(inverses, lower_parts)]
+    inverses = [t[0] for t in inverses]
     for inverse, (for_w, for_u, for_state, last), (x_ref, b, which) in zip(inverses, scales, units):
         key = x_ref[b, :N]
-        hi, lo = split(inverse * for_w)
-        w = dot(hi, key) + dot(lo, key)
+        w = dot_stacked(stack(split(inverse * for_w)), key)
         tu = inverse * for_u
-        tu_ref[b, which] = jnp.concatenate(split(tu), axis=1)
+        tu_ref[b, which] = stack(split(tu))
         w_ref[b, which] = w
         hi, lo = split(jnp.concatenate([w, tu], axis=1) * for_state)
         both = dot_tn(key, hi) + dot_tn(key, lo)
         a_ref[b, which] = jnp.concatenate(split(jnp.where(eye, last, 0.0) - both[:, :N]), axis=1)
-        m_ref[b, which] = jnp.concatenate(split(both[:, N:]), axis=1)
+        m_ref[b, which] = stack(split(both[:, N:]))
 
 
 def solve(x0, x1):
@@ -191,12 +203,13 @@
         solve_kernel,
         grid=(CHIPS // STEP,),
         in_specs=[spec(STEP, KROWS, N)] * 2,
-        out_specs=[spec(STEP, 2, 8, N), spec(STEP, 2, N, N)] + [spec(STEP, 2, N, 2 * N)] * 3,
+        out_specs=[spec(STEP, 2, 8, N), spec(STEP, 2, N, N)] + [spec(STEP, 2, 2 * N, N)] * 2 + [spec(STEP, 2, N, 2 * N)],
         out_shape=[
             pltpu.HBM((CHIPS, 2, 8, N), F32),
             pltpu.HBM((CHIPS, 2, N, N), F32),
         ]
-        + [pltpu.HBM((CHIPS, 2, N, 2 * N), BF16)] * 3,
+        + [pltpu.HBM((CHIPS, 2, 2 * N, N), BF16)] * 2
+        + [pltpu.HBM((CHIPS, 2, N, 2 * N), BF16)],
         compiler_params=params(24),
         cost_estimate=cost(16 * 10**9, 20),
         name="solve",
@@ -224,8 +237,7 @@
         for place, which in enumerate(order):
             for s in range(SPANS):
                 value = v_ref[s, 0, place]
-                hi, lo = halves(m_ref[s, 0, which])
-                offset = dot(hi, value) + dot(lo, value)
+                offset = dot_stacked(m_ref[s, 0, which], value)
                 parts = split(state[s])
                 ph_ref[s, 0, which] = jnp.concatenate(parts, axis=0)
                 state[s] = later(halves(a_ref[s, 0, which]), offset, parts)
@@ -252,11 +264,11 @@
     def of_pair(*shape):
         return pl.BlockSpec((SPANS, 1) + shape, lambda i: (0, i) + (0,) * len(shape))
 
-    m, a = (x.reshape(SPANS, PAIRS, 2, N, 2 * N) for x in (m, a))
+    m, a = m.reshape(SPANS, PAIRS, 2, 2 * N, N), a.reshape(SPANS, PAIRS, 2, N, 2 * N)
     return pl.pallas_call(
         chain_kernel,
         grid=(PAIRS,),
-        in_specs=[of_pair(2, N, 2 * N)] * 2 + [of_pair(2, N, N)],
+        in_specs=[of_pair(2, 2 * N, N), of_pair(2, N, 2 * N), of_pair(2, N, N)],
         out_specs=[
             of_pair(2, 2 * N, 2 * N),
             pl.BlockSpec((SPANS, N, 2 * N), lambda i: (0, 0, 0)),
@@ -274,7 +286,7 @@
     )(*in_hbm(m, a), v.reshape(SPANS, PAIRS, 2, N, N))
 
 
-ROWSTEP = 4
+ROWSTEP = 8
 
 
 def rows_kernel(which, x_ref, v_ref, aux_ref, w_ref, tu_ref, ph_ref, r_ref, o_ref):
@@ -291,8 +303,7 @@
         decay = jnp.exp(jnp.minimum(ccol - aux_ref[b, 0:1], 0.0))
         scores = dot_nt(query, key) * norm * aux_ref[b, 1:2] * decay
         scores = jnp.where(inclusive, scores, 0.0)
-        hi, lo = halves(tu_ref[b])
-        u = dot(hi, value) + dot(lo, value)
+        u = dot_stacked(tu_ref[b], value)
         inner = dot4(split(scores), split(jnp.concatenate([w_ref[b], u], axis=1)))
         reach = split(wide * (norm * jnp.exp(ccol)) - inner[:, :N])
         both = dot4(reach, (ph_ref[b, :N], ph_ref[b, N:]))
@@ -300,28 +311,34 @@
         o_ref[b] = both[:, N:] + inner[:, N:]
 
 
-def rows(which, x, v, aux, w, tu, ph):
+def rows(which, first, count, x, v, aux, w, tu, ph):
+    def at(i):
+        return first // ROWSTEP + i
+
+    def some(*shape):
+        return pl.BlockSpec((ROWSTEP,) + shape, lambda i: (at(i),) + (0,) * len(shape))
+
     def one_of(*shape):
-        return pl.BlockSpec((ROWSTEP, None) + shape, lambda i: (i, which) + (0,) * len(shape))
+        return pl.BlockSpec((ROWSTEP, None) + shape, lambda i: (at(i), which) + (0,) * len(shape))
 
     return pl.pallas_call(
         functools.partial(rows_kernel, which),
-        grid=(CHIPS // ROWSTEP,),
+        grid=(count // ROWSTEP,),
         in_specs=[
-            spec(ROWSTEP, KROWS, N),
-            spec(ROWSTEP, 2, N, N),
+            some(KROWS, N),
+            some(2, N, N),
             one_of(8, N),
             one_of(N, N),
-            one_of(N, 2 * N),
+            one_of(2 * N, N),
             one_of(2 * N, 2 * N),
         ],
         out_specs=[spec(ROWSTEP, N, 2 * N), spec(ROWSTEP, N, N)],
         out_shape=[
-            jax.ShapeDtypeStruct((CHIPS, N, 2 * N), BF16),
-            jax.ShapeDtypeStruct((CHIPS, N, N), F32),
+            jax.ShapeDtypeStruct((count, N, 2 * N), BF16),
+            jax.ShapeDtypeStruct((count, N, N), F32),
         ],
-        compiler_params=params(16),
-        cost_estimate=cost(5 * 10**9, 8),
+        compiler_params=params(20),
+        cost_estimate=cost(count * 3 * 10**8, count // 2),
         name="rows",
     )(x, v.reshape(CHIPS, 2, N, N), aux, w, tu, ph.reshape(CHIPS, 2, 2 * N, 2 * N))
 
@@ -350,7 +367,7 @@
     )(*args)
 
 
-def finish_kernel(got_ref, longer_ref, start_ref, r0, o0, r1, o1, out_ref, state):
+def finish_kernel(got_ref, longer_ref, start_ref, r0, o0, r1, o1, r2, o2, out_ref, state):
     step = pl.program_id(0)
 
     @pl.when(step == 0)
@@ -368,13 +385,32 @@
 
     rhs = state[step]
     core = core_here()
-    for b in range(PAIRS):
-        for place, r_ref, o_ref in ((core, r0, o0), (1 - core, r1, o1)):
+
+    def write(place, r_ref, o_ref):
+        for b in range(PAIRS):
             out = dot4(halves(r_ref[b]), (rhs[:N], rhs[N:])) + o_ref[b]
             out_ref[b, place] = out.astype(BF16)
 
-
-def finish(got, longer, start, r0, o0, r1, o1):
+    write(core, r0, o0)
+
+    @pl.when(step < SPANS // 2)
+    def _():
+        write(1 - core, r1, o1)
+
+    @pl.when(step >= SPANS // 2)
+    def _():
+        write(1 - core, r2, o2)
+
+
+def finish(got, longer, start, parts):
+    half = SPANS // 2
+
+    def pieces(index):
+        return [
+            pl.BlockSpec((PAIRS, N, 2 * N), lambda i: (index(i), 0, 0)),
+            pl.BlockSpec((PAIRS, N, N), lambda i: (index(i), 0, 0)),
+        ]
+
     return pl.pallas_call(
         finish_kernel,
         grid=(SPANS,),
@@ -383,17 +419,19 @@
             pl.BlockSpec((N, 2 * N), lambda i: (0, 0)),
             pl.BlockSpec((SPANS, N, 2 * N), lambda i: (0, 0, 0)),
         ]
-        + [spec(PAIRS, N, 2 * N), spec(PAIRS, N, N)] * 2,
+        + pieces(lambda i: i)
+        + pieces(lambda i: jnp.minimum(i, half - 1))
+        + pieces(lambda i: jnp.maximum(i - half, 0)),
         out_specs=spec(PAIRS, 2, N, N),
         out_shape=jax.ShapeDtypeStruct((CHIPS, 2, N, N), BF16),
         scratch_shapes=[pltpu.VMEM((SPANS, 2 * N, N), BF16)],
         compiler_params=params(16),
         cost_estimate=cost(10**9, 5),
         name="finish",
-    )(got, longer, start, r0, o0, r1, o1)
-
-
-PACKSTEP = 32
+    )(got, longer, start, *parts)
+
+
+PACKSTEP = 64
 
 
 def pack_kernel(k_ref, q_ref, beta_ref, gate_ref, out_ref, wide):
@@ -451,12 +489,17 @@
     v = exchange(values, EVERY)
     aux, w, tu, m, a = solve(x0, x1)
     ph, start, total = chain(m, a, v)
-    before, run = joined(first_join_kernel, (2 * N, 2 * N), onward(total, 1), total)
-    longer, offset = joined(second_join_kernel, (2 * N, N), onward(run, 2), before, run)
-    got = onward(offset, 4)
-    r0, o0 = rows(0, x0, v, aux, w, tu, ph)
-    r1, o1 = rows(1, x1, v, aux, w, tu, ph)
-    out = finish(got, longer, start, r0, o0, r1, o1)
+    hold = lax.optimization_barrier
+    made = (v, aux, w, tu, ph)
+    half = CHIPS // 2
+    got, part1 = hold((onward(total, 1), rows(1, 0, half, x1, *made)))
+    before, run = joined(first_join_kernel, (2 * N, 2 * N), got, total)
+    x0, run = hold((x0, run))
+    got, part0 = hold((onward(run, 2), rows(0, 0, CHIPS, x0, *made)))
+    longer, offset = joined(second_join_kernel, (2 * N, N), got, before, run)
+    x1, offset = hold((x1, offset))
+    part2 = rows(1, half, half, x1, *made)
+    out = finish(onward(offset, 4), longer, start, [*part0, *part1, *part2])
     return exchange(out.reshape(2 * CHIPS, N, N), EVERY).transpose(1, 0, 2)
 
 

time: 118 us -> 114 us (0.966)
  waiting for transfers between devices: 23.9 us -> 20.8 us
  Pallas kernels: 45.8 us -> 42.7 us
  blocking collectives: 24.3 us -> 26 us
    ppermute x3, waiting for transfers between devices: 9.18 us -> 6.08 us  [onward(): return lax.ppermute(x, 'ctx', ring)]
    pallas_call x1, Pallas kernels: 18.6 us -> 16.9 us  [solve(): pl.pallas_call(solve_kernel, grid=(CHIPS // STEP,), in_specs=[spec(STEP,...]
    all_to_all x1, blocking collectives: 24.3 us -> 26 us  [exchange(): lax.all_to_all(x, ('ctx', 'head'), 0, 0, tiled=True, axis_index_groups=gr...]
    pallas_call x3 -> x4, Pallas kernels: 20.9 us -> 19.7 us  [the longest x3 14.2 us: rows(): pl.pallas_call(functools.partial(rows_kernel, which), grid=(count // ROWS...]
  transfers between devices with their start and end apart: 6 -> 6, of which waited for: 3 -> 3; matrix products, arithmetic and copies ran while one was open for 1% -> 1% of each run, Pallas kernels for 29% -> 27%
where the time goes in v3:
time: 114 us; the launch traced here: 113 us
  Pallas kernels  42.7 us (37%)
  blocking collectives  26 us (23%)
  waiting for transfers between devices  20.8 us (18%)
  starting transfers between devices  20.5 us (18%)
  local copies, waits for them, and re-layouts  3.04 us (3%)
    all_to_all x1, blocking collectives, exchange(): lax.all_to_all(x, ('ctx', 'head'), 0, 0, tiled=True, axis_index_groups=gr...  26 us
    pallas_call x1, Pallas kernels, solve(): pl.pallas_call(solve_kernel, grid=(CHIPS // STEP,), in_specs=[spec(STEP,...  16.9 us
    all_to_all x2, waiting for transfers between devices, exchange(): lax.all_to_all(x, ('ctx', 'head'), 0, 0, tiled=True, axis_index_groups=gr...  14.7 us
    pallas_call x3, Pallas kernels, rows(): pl.pallas_call(functools.partial(rows_kernel, which), grid=(count // ROWS...  14.2 us
    all_to_all x2, starting transfers between devices, exchange(): lax.all_to_all(x, ('ctx', 'head'), 0, 0, tiled=True, axis_index_groups=gr...  11.3 us
    ppermute x3, waiting for transfers between devices, onward(): return lax.ppermute(x, 'ctx', ring)  6.08 us
    ppermute x3, starting transfers between devices, onward(): return lax.ppermute(x, 'ctx', ring)  5.84 us
    pallas_call x1, Pallas kernels, chain(): pl.pallas_call(chain_kernel, grid=(PAIRS,), in_specs=[of_pair(2, 2 * N, N...  5.51 us
  transfers between devices with their start and end apart: 6, of which 3 were waited for; matrix products, arithmetic and copies ran while one was open for 1% of the time, Pallas kernels for 27%

profile of v3, /device:TPU:1, one launch (start us, length us, event | category | flops | bytes accessed | tf_op | source)
XLA Modules:
  0.0 113.2 jit_solution(2739618657648536521)
XLA Ops:
  0.0 0.0 copy-start.3
  0.0 2.9 %pack.1 = bf16[16,272,128]{2,1,0:T(8,128)(2,1)} custom-call(bf16[128,16,128]{2,1,0:T(8,128)(2,1)} %k_ref.1, bf16[128,16,128]{2,1,0:T(8,128)(2,1)} %q_ref.1, bf16[32,128]{1,0:T(8,128)(2,1)} %bitcast.22, bf16[32,128]{1,0:T(8,128)(2,1)} %bitcast.23), custom_call_target="tpu_custom_call" | custom-call | tf_op jit(solution)/shard_map/pack/pallas_call | solution.py:456
  2.9 7.6 %all-to-all-start = ((bf16[16,272,128]{2,1,0:T(8,128)(2,1)}), bf16[16,272,128]{2,1,0:T(8,128)(2,1)S(1)}, u32[]{:S(2)}, u32[]{:S(2)}) async-start(bf16[16,272,128]{2,1,0:T(8,128)(2,1)} %pack.1), calls=%async_computation | async-start | bytes 2228224 | tf_op jit(solution)/shard_map/all_to_all | solution.py:473
  10.5 0.0 copy-done.3
  10.5 1.4 %copy.12 = bf16[128,32,128]{2,0,1:T(8,128)(2,1)} copy(bf16[128,32,128]{2,1,0:T(8,128)(2,1)S(1)} %copy-done.3) | data formatting | bytes 2097152 | tf_op args[2]
  11.9 14.7 %all-to-all-done.x0_ref.x_ref = bf16[16,272,128]{2,1,0:T(8,128)(2,1)S(1)} async-done(((bf16[16,272,128]{2,1,0:T(8,128)(2,1)}), bf16[16,272,128]{2,1,0:T(8,128)(2,1)S(1)}, u32[]{:S(2)}, u32[]{:S(2)}) %all-to-all-start) | async-done | bytes 1114144 | tf_op jit(solution)/shard_map/all_to_all | solution.py:473
  26.6 3.4 %collective-permute-start = (bf16[16,272,128]{2,1,0:T(8,128)(2,1)S(1)}, bf16[16,272,128]{2,1,0:T(8,128)(2,1)S(1)}, u32[]{:S(2)}, u32[]{:S(2)}) collective-permute-start(bf16[16,272,128]{2,1,0:T(8,128)(2,1)S(1)} %all-to-all-done.x0_ref.x_ref), channel_id=1, source_target_pairs={{0,1},{1,0},{2,3},{3,2},{4,5},{5,4},{6,7},{7,6},{8,9},{9,8},{10,11... | collective-permute-start | bytes 3342344 | tf_op jit(solution)/shard_map/ppermute | solution.py:482
  30.0 3.7 %all-to-all-start.1 = ((bf16[32,128,128]{2,1,0:T(8,128)(2,1)}), bf16[32,128,128]{2,1,0:T(8,128)(2,1)S(1)}, u32[]{:S(2)}, u32[]{:S(2)}) async-start(bf16[32,128,128]{2,1,0:T(8,128)(2,1)} %bitcast.20), calls=%async_computation.1 | async-start | bytes 2097152 | tf_op jit(solution)/shard_map/all_to_all | solution.py:473
  33.7 0.0 collective-permute-done.x1_ref.x_ref
  33.7 16.9 %solve.1 = (f32[16,2,8,128]{3,2,1,0:T(8,128)}, f32[16,2,128,128]{3,2,1,0:T(8,128)}, bf16[16,2,256,128]{3,2,1,0:T(8,128)(2,1)}, bf16[16,2,256,128]{3,2,1,0:T(8,128)(2,1)}, bf16[16,2,128,256]{3,2,1,0:T(8,128)(2,1)}) custom-call(bf16[16,272,128]{2,1,0:T(8,128)(2,1)S(1)} %all-to-all-done.x0_ref.x_ref, bf16[16,272,128]{2,1,0:T(8,128)(2,1)S(1)} %collective-permute-done.x1_ref.x_ref), custom_call_target="tpu_custom_call" | custom-call | flops 16000000000 | bytes 20971520 | tf_op jit(solution)/shard_map/solve/pallas_call | solution.py:202
  50.6 0.0 all-to-all-done.1
  50.6 0.0 copy-start
  50.6 0.0 copy-start.1
  50.6 0.0 copy-start.2
  50.6 5.5 %chain.1 = (bf16[4,4,2,256,256]{4,3,2,1,0:T(8,128)(2,1)S(1)}, f32[4,128,256]{2,1,0:T(8,128)S(1)}, f32[128,256]{1,0:T(8,128)S(1)}) custom-call(bf16[4,4,2,256,128]{4,3,2,1,0:T(8,128)(2,1)} %bitcast.24, bf16[4,4,2,128,256]{4,3,2,1,0:T(8,128)(2,1)} %bitcast.25, bf16[4,4,2,128,128]{4,3,2,1,0:T(8,128)(2,1)S(1)} %bitcast.15), custom_call_target="tpu_custom_call" | custom-call | flops 4000000000 | bytes 10485760 | tf_op jit(solution)/shard_map/chain/pallas_call | solution.py:268
  56.2 1.7 %collective-permute-start.1 = (f32[128,256]{1,0:T(8,128)S(1)}, f32[128,256]{1,0:T(8,128)S(1)}, u32[]{:S(2)}, u32[]{:S(2)}) collective-permute-start(f32[128,256]{1,0:T(8,128)S(1)} %get-tuple-element.39.own_ref), channel_id=1, source_target_pairs={{0,32},{8,40},{16,48},{24,56},{32,64},{40,72},{48,80},{56,88},{64,... | collective-permute-start | bytes 393224 | tf_op jit(solution)/shard_map/ppermute | solution.py:478
  57.9 0.0 copy-done
  57.9 0.0 copy-done.1
  57.9 0.0 copy-done.2
  57.9 3.5 %rows.3 = (bf16[8,128,256]{2,1,0:T(8,128)(2,1)S(1)}, f32[8,128,128]{2,1,0:T(8,128)S(1)}) custom-call(bf16[16,272,128]{2,1,0:T(8,128)(2,1)S(1)} %collective-permute-done.x1_ref.x_ref, bf16[16,2,128,128]{3,2,1,0:T(8,128)(2,1)S(1)} %bitcast.16, f32[16,2,8,128]{3,2,1,0:T(8,128)S(1)} %copy-done.2, f32[16,2,128,128]{3,2,1,0:T(8,128)S(1)} %copy-done, ...), custom_call_target="tpu_custom_call" | custom-call | flops 2400000000 | bytes 4194304 | tf_op jit(solution)/shard_map/rows/pallas_call | solution.py:324
  61.4 4.2 %collective-permute-done.1.got_ref = f32[128,256]{1,0:T(8,128)S(1)} collective-permute-done((f32[128,256]{1,0:T(8,128)S(1)}, f32[128,256]{1,0:T(8,128)S(1)}, u32[]{:S(2)}, u32[]{:S(2)}) %collective-permute-start.1) | collective-permute-done | bytes 131104 | tf_op jit(solution)/shard_map/ppermute | solution.py:478
  65.6 0.2 shard_map.55
  65.8 0.1 collective-permute-start.2
  65.9 7.3 %rows.4 = (bf16[16,128,256]{2,1,0:T(8,128)(2,1)S(1)}, f32[16,128,128]{2,1,0:T(8,128)S(1)}) custom-call(bf16[16,272,128]{2,1,0:T(8,128)(2,1)S(1)} %all-to-all-done.x0_ref.x_ref, bf16[16,2,128,128]{3,2,1,0:T(8,128)(2,1)S(1)} %bitcast.17, f32[16,2,8,128]{3,2,1,0:T(8,128)S(1)} %copy-done.2, f32[16,2,128,128]{3,2,1,0:T(8,128)S(1)} %copy-done, ...), custom_call_target="tpu_custom_call" | custom-call | flops 4800000000 | bytes 8388608 | tf_op jit(solution)/shard_map/rows/pallas_call | solution.py:324
  73.1 1.9 %collective-permute-done.2.got_ref = f32[128,256]{1,0:T(8,128)S(1)} collective-permute-done((f32[128,256]{1,0:T(8,128)S(1)}, f32[128,256]{1,0:T(8,128)S(1)}, u32[]{:S(2)}, u32[]{:S(2)}) %collective-permute-start.2) | collective-permute-done | bytes 131104 | tf_op jit(solution)/shard_map/ppermute | solution.py:478
  75.0 0.2 shard_map.56
  75.2 4.0 %collective-permute-start.3 = (f32[128,128]{1,0:T(8,128)S(1)}, f32[128,128]{1,0:T(8,128)S(1)}, u32[]{:S(2)}, u32[]{:S(2)}) collective-permute-start(f32[128,128]{1,0:T(8,128)S(1)} %get-tuple-element.55), channel_id=1, source_target_pairs={{0,128},{8,136},{16,144},{24,152},{32,160},{40,168},{48,176},{56,1... | collective-permute-start | bytes 196616 | tf_op jit(solution)/shard_map/ppermute | solution.py:478
  79.3 3.5 %rows.5 = (bf16[8,128,256]{2,1,0:T(8,128)(2,1)S(1)}, f32[8,128,128]{2,1,0:T(8,128)S(1)}) custom-call(bf16[16,272,128]{2,1,0:T(8,128)(2,1)S(1)} %collective-permute-done.x1_ref.x_ref, bf16[16,2,128,128]{3,2,1,0:T(8,128)(2,1)S(1)} %bitcast.18, f32[16,2,8,128]{3,2,1,0:T(8,128)S(1)} %copy-done.2, f32[16,2,128,128]{3,2,1,0:T(8,128)S(1)} %copy-done, ...), custom_call_target="tpu_custom_call" | custom-call | flops 2400000000 | bytes 4194304 | tf_op jit(solution)/shard_map/rows/pallas_call | solution.py:324
  82.7 0.0 collective-permute-done.3.got_ref
  82.7 2.8 %finish.1 = bf16[16,2,128,128]{3,2,1,0:T(8,128)(2,1)S(1)} custom-call(f32[128,128]{1,0:T(8,128)S(1)} %collective-permute-done.3.got_ref, f32[128,256]{1,0:T(8,128)S(1)} %get-tuple-element.56.longer_ref, f32[4,128,256]{2,1,0:T(8,128)S(1)} %get-tuple-element.57.start_ref, bf16[16,128,256]{2,1,0:T(8,128)(2,1)S(1)} %get-tuple-element.58.r0, ...), custom_call_target="tpu_custom_call" | custom-call | flops 1000000000 | bytes 5242880 | tf_op jit(solution)/shard_map/finish/pallas_call | solution.py:414
  85.5 26.0 %all_to_all.15 = bf16[32,128,128]{2,1,0:T(8,128)(2,1)S(1)} all-to-all(bf16[32,128,128]{2,1,0:T(8,128)(2,1)S(1)} %bitcast.19), channel_id=1, replica_groups={{0,1,2,3,4,5,6,7,8,9,10,11,12,13,14,15,16,17,18,19,20,21,22,23,24,25,26..., dimensions={0} | all-to-all | bytes 2097152 | tf_op jit(solution)/shard_map/all_to_all | solution.py:473
  111.5 1.6 %copy.10 = bf16[128,32,128]{2,1,0:T(8,128)(2,1)} copy(bf16[128,32,128]{2,0,1:T(8,128)(2,1)S(1)} %bitcast.21) | data formatting | bytes 2097152 | tf_op jit(solution)/shard_map/transpose | solution.py:503
Async XLA Ops:
  0.0 10.5 %copy-start.3 = (bf16[128,32,128]{2,1,0:T(8,128)(2,1)S(1)}, bf16[128,32,128]{2,1,0:T(8,128)(2,1)}, u32[]{:S(2)}) copy-start(bf16[128,32,128]{2,1,0:T(8,128)(2,1)} %param.7) | copy-start | bytes 3145732
  2.9 23.7 %all-to-all-start = ((bf16[16,272,128]{2,1,0:T(8,128)(2,1)}), bf16[16,272,128]{2,1,0:T(8,128)(2,1)S(1)}, u32[]{:S(2)}, u32[]{:S(2)}) async-start(bf16[16,272,128]{2,1,0:T(8,128)(2,1)} %pack.1), calls=%async_computation | async-start | bytes 2228224 | tf_op jit(solution)/shard_map/all_to_all | solution.py:473
  26.6 7.1 %collective-permute-start = (bf16[16,272,128]{2,1,0:T(8,128)(2,1)S(1)}, bf16[16,272,128]{2,1,0:T(8,128)(2,1)S(1)}, u32[]{:S(2)}, u32[]{:S(2)}) collective-permute-start(bf16[16,272,128]{2,1,0:T(8,128)(2,1)S(1)} %all-to-all-done.x0_ref.x_ref), channel_id=1, source_target_pairs={{0,1},{1,0},{2,3},{3,2},{4,5},{5,4},{6,7},{7,6},{8,9},{9,8},{10,11... | collective-permute-start | bytes 3342344 | tf_op jit(solution)/shard_map/ppermute | solution.py:482
  30.0 20.6 %all-to-all-start.1 = ((bf16[32,128,128]{2,1,0:T(8,128)(2,1)}), bf16[32,128,128]{2,1,0:T(8,128)(2,1)S(1)}, u32[]{:S(2)}, u32[]{:S(2)}) async-start(bf16[32,128,128]{2,1,0:T(8,128)(2,1)} %bitcast.20), calls=%async_computation.1 | async-start | bytes 2097152 | tf_op jit(solution)/shard_map/all_to_all | solution.py:473
  50.6 7.3 %copy-start = (f32[16,2,128,128]{3,2,1,0:T(8,128)S(1)}, f32[16,2,128,128]{3,2,1,0:T(8,128)}, u32[]{:S(2)}) copy-start(f32[16,2,128,128]{3,2,1,0:T(8,128)} %get-tuple-element.41.w_ref) | copy-start | bytes 6291460
  50.6 7.3 %copy-start.1 = (bf16[16,2,256,128]{3,2,1,0:T(8,128)(2,1)S(1)}, bf16[16,2,256,128]{3,2,1,0:T(8,128)(2,1)}, u32[]{:S(2)}) copy-start(bf16[16,2,256,128]{3,2,1,0:T(8,128)(2,1)} %get-tuple-element.42.tu_ref) | copy-start | bytes 6291460
  50.6 7.3 %copy-start.2 = (f32[16,2,8,128]{3,2,1,0:T(8,128)S(1)}, f32[16,2,8,128]{3,2,1,0:T(8,128)}, u32[]{:S(2)}) copy-start(f32[16,2,8,128]{3,2,1,0:T(8,128)} %get-tuple-element.40.aux_ref) | copy-start | bytes 393220
  56.2 9.4 %collective-permute-start.1 = (f32[128,256]{1,0:T(8,128)S(1)}, f32[128,256]{1,0:T(8,128)S(1)}, u32[]{:S(2)}, u32[]{:S(2)}) collective-permute-start(f32[128,256]{1,0:T(8,128)S(1)} %get-tuple-element.39.own_ref), channel_id=1, source_target_pairs={{0,32},{8,40},{16,48},{24,56},{32,64},{40,72},{48,80},{56,88},{64,... | collective-permute-start | bytes 393224 | tf_op jit(solution)/shard_map/ppermute | solution.py:478
  65.8 9.2 %collective-permute-start.2 = (f32[128,256]{1,0:T(8,128)S(1)}, f32[128,256]{1,0:T(8,128)S(1)}, u32[]{:S(2)}, u32[]{:S(2)}) collective-permute-start(f32[128,256]{1,0:T(8,128)S(1)} %get-tuple-element.48.run_ref), channel_id=1, source_target_pairs={{0,64},{8,72},{16,80},{24,88},{32,96},{40,104},{48,112},{56,120},{... | collective-permute-start | bytes 393224 | tf_op jit(solution)/shard_map/ppermute | solution.py:478
  75.2 7.5 %collective-permute-start.3 = (f32[128,128]{1,0:T(8,128)S(1)}, f32[128,128]{1,0:T(8,128)S(1)}, u32[]{:S(2)}, u32[]{:S(2)}) collective-permute-start(f32[128,128]{1,0:T(8,128)S(1)} %get-tuple-element.55), channel_id=1, source_target_pairs={{0,128},{8,136},{16,144},{24,152},{32,160},{40,168},{48,176},{56,1... | collective-permute-start | bytes 196616 | tf_op jit(solution)/shard_map/ppermute | solution.py:478

commit v4 on v3

--- a/solution.py
+++ b/solution.py
@@ -11,8 +11,9 @@
 CHIPS = 16
 SPANS = 4
 PAIRS = 4
-Q0, G0 = N, 2 * N
-KROWS = 2 * N + 16
+G0 = N
+VROWS = N + N // 2
+KROWS = N + 16
 F32, BF16 = jnp.float32, jnp.bfloat16
 
 
@@ -236,7 +237,7 @@
     def advance(order):
         for place, which in enumerate(order):
             for s in range(SPANS):
-                value = v_ref[s, 0, place]
+                value = v_ref[s, 0, place, :N]
                 offset = dot_stacked(m_ref[s, 0, which], value)
                 parts = split(state[s])
                 ph_ref[s, 0, which] = jnp.concatenate(parts, axis=0)
@@ -268,7 +269,7 @@
     return pl.pallas_call(
         chain_kernel,
         grid=(PAIRS,),
-        in_specs=[of_pair(2, 2 * N, N), of_pair(2, N, 2 * N), of_pair(2, N, N)],
+        in_specs=[of_pair(2, 2 * N, N), of_pair(2, N, 2 * N), of_pair(2, VROWS, N)],
         out_specs=[
             of_pair(2, 2 * N, 2 * N),
             pl.BlockSpec((SPANS, N, 2 * N), lambda i: (0, 0, 0)),
@@ -283,54 +284,89 @@
         compiler_params=params(16),
         cost_estimate=cost(4 * 10**9, 10),
         name="chain",
-    )(*in_hbm(m, a), v.reshape(SPANS, PAIRS, 2, N, N))
-
-
+    )(*in_hbm(m, a), v.reshape(SPANS, PAIRS, 2, VROWS, N))
+
+
+PRESTEP = 4
 ROWSTEP = 8
 
 
-def rows_kernel(which, x_ref, v_ref, aux_ref, w_ref, tu_ref, ph_ref, r_ref, o_ref):
+def before_queries_kernel(v_ref, w_ref, tu_ref, ph_ref, e_ref):
+    core = core_here()
+    for b in range(PRESTEP):
+        for which in range(2):
+            value = v_ref[b, core if which == 0 else 1 - core, :N]
+            u = dot_stacked(tu_ref[b, which], value)
+            ph = ph_ref[b, which]
+            moved = dot4(split(w_ref[b, which]), (ph[:N], ph[N:]))
+            errors = jnp.concatenate([-moved[:, :N], u - moved[:, N:]], axis=1)
+            e_ref[b, which] = stack(split(errors))
+
+
+def before_queries(first, count, v, w, tu, ph):
+    def some(*shape):
+        return pl.BlockSpec(
+            (PRESTEP, 2) + shape, lambda i: (first // PRESTEP + i,) + (0,) * (len(shape) + 1)
+        )
+
+    return pl.pallas_call(
+        before_queries_kernel,
+        grid=(count // PRESTEP,),
+        in_specs=[some(VROWS, N), some(N, N), some(2 * N, N), some(2 * N, 2 * N)],
+        out_specs=spec(PRESTEP, 2, 2 * N, 2 * N),
+        out_shape=jax.ShapeDtypeStruct((count, 2, 2 * N, 2 * N), BF16),
+        compiler_params=params(20),
+        cost_estimate=cost(count * 3 * 10**8, count // 2),
+        name="before_queries",
+    )(v.reshape(CHIPS, 2, VROWS, N), w, tu, ph)
+
+
+def rows_kernel(which, x_ref, v_ref, q_ref, aux_ref, e_ref, ph_ref, r_ref, o_ref):
     core = core_here()
     first = core == 0
     place = core if which == 0 else 1 - core
     inclusive = iota((N, N), 0) >= iota((N, N), 1)
     for b in range(ROWSTEP):
-        key, query, value = x_ref[b, :N], x_ref[b, Q0 : Q0 + N], v_ref[b, place]
+        key = x_ref[b, :N]
+        here, there = v_ref[b, place, N:].astype(F32), q_ref[b, place].astype(F32)
+        wide = jnp.concatenate(
+            [jnp.where(first, here, there), jnp.where(first, there, here)], axis=0
+        )
+        query = wide.astype(BF16)
         cols_here, _ = gate_columns(x_ref[b, G0 : G0 + 16])
         ccol = jnp.where(first, cols_here[:, 2:3], cols_here[:, 3:4])
-        wide = query.astype(F32)
         norm = lax.rsqrt(jnp.sum(wide * wide, axis=1, keepdims=True) + 1e-06) * N ** (-0.5)
         decay = jnp.exp(jnp.minimum(ccol - aux_ref[b, 0:1], 0.0))
         scores = dot_nt(query, key) * norm * aux_ref[b, 1:2] * decay
         scores = jnp.where(inclusive, scores, 0.0)
-        u = dot_stacked(tu_ref[b], value)
-        inner = dot4(split(scores), split(jnp.concatenate([w_ref[b], u], axis=1)))
-        reach = split(wide * (norm * jnp.exp(ccol)) - inner[:, :N])
-        both = dot4(reach, (ph_ref[b, :N], ph_ref[b, N:]))
+        carried = dot(jnp.concatenate([query, query], axis=1), ph_ref[b])
+        both = dot4(split(scores), (e_ref[b, :N], e_ref[b, N:])) + carried * (norm * jnp.exp(ccol))
         r_ref[b] = jnp.concatenate(split(both[:, :N]), axis=1)
-        o_ref[b] = both[:, N:] + inner[:, N:]
-
-
-def rows(which, first, count, x, v, aux, w, tu, ph):
-    def at(i):
-        return first // ROWSTEP + i
+        o_ref[b] = both[:, N:]
+
+
+def rows(which, x, v, q, aux, e, ph):
+    first, count = 0, CHIPS
 
     def some(*shape):
-        return pl.BlockSpec((ROWSTEP,) + shape, lambda i: (at(i),) + (0,) * len(shape))
-
-    def one_of(*shape):
-        return pl.BlockSpec((ROWSTEP, None) + shape, lambda i: (at(i), which) + (0,) * len(shape))
+        return pl.BlockSpec((ROWSTEP,) + shape, lambda i: (first // ROWSTEP + i,) + (0,) * len(shape))
+
+    def one_of(start, *shape):
+        return pl.BlockSpec(
+            (ROWSTEP, None) + shape,
+            lambda i: (start // ROWSTEP + i, which) + (0,) * len(shape),
+        )
 
     return pl.pallas_call(
         functools.partial(rows_kernel, which),
         grid=(count // ROWSTEP,),
         in_specs=[
             some(KROWS, N),
-            some(2, N, N),
-            one_of(8, N),
-            one_of(N, N),
-            one_of(2 * N, N),
-            one_of(2 * N, 2 * N),
+            some(2, VROWS, N),
+            some(2, N // 2, N),
+            one_of(first, 8, N),
+            one_of(0, 2 * N, 2 * N),
+            one_of(first, 2 * N, 2 * N),
         ],
         out_specs=[spec(ROWSTEP, N, 2 * N), spec(ROWSTEP, N, N)],
         out_shape=[
@@ -340,7 +376,7 @@
         compiler_params=params(20),
         cost_estimate=cost(count * 3 * 10**8, count // 2),
         name="rows",
-    )(x, v.reshape(CHIPS, 2, N, N), aux, w, tu, ph.reshape(CHIPS, 2, 2 * N, 2 * N))
+    )(x, v.reshape(CHIPS, 2, VROWS, N), q.reshape(CHIPS, 2, N // 2, N), aux, e, ph)
 
 
 def first_join_kernel(got_ref, own_ref, before_ref, run_ref):
@@ -367,7 +403,7 @@
     )(*args)
 
 
-def finish_kernel(got_ref, longer_ref, start_ref, r0, o0, r1, o1, r2, o2, out_ref, state):
+def finish_kernel(got_ref, longer_ref, start_ref, r0, o0, r1, o1, out_ref, state):
     step = pl.program_id(0)
 
     @pl.when(step == 0)
@@ -392,25 +428,10 @@
             out_ref[b, place] = out.astype(BF16)
 
     write(core, r0, o0)
-
-    @pl.when(step < SPANS // 2)
-    def _():
-        write(1 - core, r1, o1)
-
-    @pl.when(step >= SPANS // 2)
-    def _():
-        write(1 - core, r2, o2)
+    write(1 - core, r1, o1)
 
 
 def finish(got, longer, start, parts):
-    half = SPANS // 2
-
-    def pieces(index):
-        return [
-            pl.BlockSpec((PAIRS, N, 2 * N), lambda i: (index(i), 0, 0)),
-            pl.BlockSpec((PAIRS, N, N), lambda i: (index(i), 0, 0)),
-        ]
-
     return pl.pallas_call(
         finish_kernel,
         grid=(SPANS,),
@@ -419,9 +440,7 @@
             pl.BlockSpec((N, 2 * N), lambda i: (0, 0)),
             pl.BlockSpec((SPANS, N, 2 * N), lambda i: (0, 0, 0)),
         ]
-        + pieces(lambda i: i)
-        + pieces(lambda i: jnp.minimum(i, half - 1))
-        + pieces(lambda i: jnp.maximum(i - half, 0)),
+        + 2 * [spec(PAIRS, N, 2 * N), spec(PAIRS, N, N)],
         out_specs=spec(PAIRS, 2, N, N),
         out_shape=jax.ShapeDtypeStruct((CHIPS, 2, N, N), BF16),
         scratch_shapes=[pltpu.VMEM((SPANS, 2 * N, N), BF16)],
@@ -434,14 +453,13 @@
 PACKSTEP = 64
 
 
-def pack_kernel(k_ref, q_ref, beta_ref, gate_ref, out_ref, wide):
+def pack_kernel(k_ref, beta_ref, gate_ref, out_ref, wide):
     step = pl.program_id(0)
-    for start, ref in ((0, k_ref), (Q0, q_ref)):
-        wide[start // N] = ref[...].astype(F32).reshape(16 * PACKSTEP, N)
-        row = pl.multiple_of(start + step * PACKSTEP, PACKSTEP)
-        for h in range(16):
-            rows = wide[start // N, pl.ds(h, PACKSTEP, stride=16), :]
-            out_ref[h, pl.ds(row, PACKSTEP), :] = rows.astype(BF16)
+    wide[...] = k_ref[...].astype(F32).reshape(16 * PACKSTEP, N)
+    row = pl.multiple_of(step * PACKSTEP, PACKSTEP)
+    for h in range(16):
+        rows = wide[pl.ds(h, PACKSTEP, stride=16), :]
+        out_ref[h, pl.ds(row, PACKSTEP), :] = rows.astype(BF16)
 
     @pl.when(step == 0)
     def _():
@@ -452,17 +470,17 @@
             out_ref[h, G0:] = tail.astype(BF16)
 
 
-def pack(key_rows, query_rows, beta_rows, log_gate):
+def pack(key_rows, beta_rows, log_gate):
     return pl.pallas_call(
         pack_kernel,
         grid=(N // PACKSTEP,),
-        in_specs=[spec(PACKSTEP, 16, N)] * 2 + [pl.BlockSpec((32, N), lambda i: (0, 0))] * 2,
+        in_specs=[spec(PACKSTEP, 16, N)] + [pl.BlockSpec((32, N), lambda i: (0, 0))] * 2,
         out_specs=pl.BlockSpec((CHIPS, KROWS, N), lambda i: (0, 0, 0)),
         out_shape=jax.ShapeDtypeStruct((CHIPS, KROWS, N), BF16),
-        scratch_shapes=[pltpu.VMEM((2, 16 * PACKSTEP, N), F32)],
+        scratch_shapes=[pltpu.VMEM((16 * PACKSTEP, N), F32)],
         compiler_params=params(60),
         name="pack",
-    )(key_rows, query_rows, beta_rows.T, log_gate.T)
+    )(key_rows, beta_rows.T, log_gate.T)
 
 
 EVERY = [list(range(32 * g, 32 * g + 32)) for g in range(8)]
@@ -483,23 +501,25 @@
 
 
 def local(query_rows, key_rows, value_rows, beta_rows, log_gate):
-    x0 = exchange(pack(key_rows, query_rows, beta_rows, log_gate), ALIKE)
-    values, x0 = lax.optimization_barrier((value_rows.transpose(1, 0, 2), x0))
+    hold = lax.optimization_barrier
+    x0 = exchange(pack(key_rows, beta_rows, log_gate), ALIKE)
+    halved = query_rows.transpose(1, 0, 2).reshape(2 * CHIPS, N // 2, N)
+    values = jnp.concatenate([value_rows.transpose(1, 0, 2), halved], axis=1)
+    values, x0 = hold((values, x0))
     x1 = other_core(x0)
     v = exchange(values, EVERY)
     aux, w, tu, m, a = solve(x0, x1)
     ph, start, total = chain(m, a, v)
-    hold = lax.optimization_barrier
-    made = (v, aux, w, tu, ph)
-    half = CHIPS // 2
-    got, part1 = hold((onward(total, 1), rows(1, 0, half, x1, *made)))
+    ph = ph.reshape(CHIPS, 2, 2 * N, 2 * N)
+    q = other_core(v[:, N:])
+    got, e = hold((onward(total, 1), before_queries(0, CHIPS, v, w, tu, ph)))
     before, run = joined(first_join_kernel, (2 * N, 2 * N), got, total)
     x0, run = hold((x0, run))
-    got, part0 = hold((onward(run, 2), rows(0, 0, CHIPS, x0, *made)))
+    got, part0 = hold((onward(run, 2), rows(0, x0, v, q, aux, e, ph)))
     longer, offset = joined(second_join_kernel, (2 * N, N), got, before, run)
     x1, offset = hold((x1, offset))
-    part2 = rows(1, half, half, x1, *made)
-    out = finish(onward(offset, 4), longer, start, [*part0, *part1, *part2])
+    part1 = rows(1, x1, v, q, aux, e, ph)
+    out = finish(onward(offset, 4), longer, start, [*part0, *part1])
     return exchange(out.reshape(2 * CHIPS, N, N), EVERY).transpose(1, 0, 2)
 
 

time: 114 us -> 109 us (0.956)
  Pallas kernels: 42.7 us -> 37.7 us
  blocking collectives: 26 us -> 22.4 us
  waiting for transfers between devices: 20.8 us -> 24.3 us
  other arithmetic: 0 us -> 1.34 us
    pallas_call x3 -> x2, Pallas kernels: 14.2 us -> 8.06 us  [rows(): pl.pallas_call(functools.partial(rows_kernel, which), grid=(count // ROWS...]
    ppermute x3, waiting for transfers between devices: 6.08 us -> 10.8 us  [onward(): return lax.ppermute(x, 'ctx', ring)]
    all_to_all x1, blocking collectives: 26 us -> 22.4 us  [exchange(): lax.all_to_all(x, ('ctx', 'head'), 0, 0, tiled=True, axis_index_groups=gr...]
    pallas_call x0 -> x1, Pallas kernels: none -> 2.38 us  [before_queries(): pl.pallas_call(before_queries_kernel, grid=(count // PRESTEP,), in_specs=...]
    concatenate x0 -> x1, other arithmetic: none -> 1.34 us  [local(): values = jnp.concatenate([value_rows.transpose(1, 0, 2), halved], axis=1)]
    all_to_all x2, waiting for transfers between devices: 14.7 us -> 13.5 us  [exchange(): lax.all_to_all(x, ('ctx', 'head'), 0, 0, tiled=True, axis_index_groups=gr...]
    ppermute x1 -> x2, starting transfers between devices: 3.39 us -> 2.8 us  [other_core(): return lax.ppermute(x, 'head', [(i, i ^ 1) for i in range(8)])]
  transfers between devices with their start and end apart: 6 -> 7, of which waited for: 3 -> 4; matrix products, arithmetic and copies ran while one was open for 1% -> 3% of each run, Pallas kernels for 27% -> 30%
where the time goes in v4:
time: 109 us
  Pallas kernels  37.7 us (35%)
  waiting for transfers between devices  24.3 us (22%)
  blocking collectives  22.4 us (21%)
  starting transfers between devices  19.7 us (18%)
  local copies, waits for them, and re-layouts  3.47 us (3%)
  other arithmetic  1.34 us (1%)
    all_to_all x1, blocking collectives, exchange(): lax.all_to_all(x, ('ctx', 'head'), 0, 0, tiled=True, axis_index_groups=gr...  22.4 us
    pallas_call x1, Pallas kernels, solve(): pl.pallas_call(solve_kernel, grid=(CHIPS // STEP,), in_specs=[spec(STEP,...  17 us
    all_to_all x2, waiting for transfers between devices, exchange(): lax.all_to_all(x, ('ctx', 'head'), 0, 0, tiled=True, axis_index_groups=gr...  13.5 us
    all_to_all x2, starting transfers between devices, exchange(): lax.all_to_all(x, ('ctx', 'head'), 0, 0, tiled=True, axis_index_groups=gr...  11.5 us
    ppermute x3, waiting for transfers between devices, onward(): return lax.ppermute(x, 'ctx', ring)  10.8 us
    pallas_call x2, Pallas kernels, rows(): pl.pallas_call(functools.partial(rows_kernel, which), grid=(count // ROWS...  8.06 us
    ppermute x3, starting transfers between devices, onward(): return lax.ppermute(x, 'ctx', ring)  5.39 us
    pallas_call x1, Pallas kernels, chain(): pl.pallas_call(chain_kernel, grid=(PAIRS,), in_specs=[of_pair(2, 2 * N, N...  5.32 us
  transfers between devices with their start and end apart: 7, of which 4 were waited for; matrix products, arithmetic and copies ran while one was open for 3% of the time, Pallas kernels for 30%

profile of v4, /device:TPU:1, one launch (start us, length us, event | category | flops | bytes accessed | tf_op | source)
XLA Modules:
  0.0 109.0 jit_solution(16681805890385741526)
XLA Ops:
  0.0 0.0 copy-start.3
  0.0 2.2 %pack.1 = bf16[16,144,128]{2,1,0:T(8,128)(2,1)} custom-call(bf16[128,16,128]{2,1,0:T(8,128)(2,1)} %k_ref.1, bf16[32,128]{1,0:T(8,128)(2,1)} %bitcast.29, bf16[32,128]{1,0:T(8,128)(2,1)} %bitcast.30), custom_call_target="tpu_custom_call" | custom-call | tf_op jit(solution)/shard_map/pack/pallas_call | solution.py:474
  2.2 7.6 %all-to-all-start = ((bf16[16,144,128]{2,1,0:T(8,128)(2,1)}), bf16[16,144,128]{2,1,0:T(8,128)(2,1)S(1)}, u32[]{:S(2)}, u32[]{:S(2)}) async-start(bf16[16,144,128]{2,1,0:T(8,128)(2,1)} %pack.1), calls=%async_computation | async-start | bytes 1179648 | tf_op jit(solution)/shard_map/all_to_all | solution.py:491
  9.8 1.6 %copy.20 = bf16[128,32,128]{2,0,1:T(8,128)(2,1)S(1)} copy(bf16[128,32,128]{2,1,0:T(8,128)(2,1)} %param.7) | data formatting | bytes 2097152 | tf_op args[2]
  11.5 0.0 copy-done.3
  11.5 0.1 copy.17
  11.6 1.3 %pad_maximum_fusion = bf16[32,192,128]{2,1,0:T(8,128)(2,1)} fusion(bf16[32,64,128]{2,1,0:T(8,128)(2,1)S(1)} %bitcast.28, bf16[32,128,128]{2,1,0:T(8,128)(2,1)S(1)} %bitcast.26), kind=kLoop, calls=%fused_computation | loop fusion | flops 3145728 | bytes 3145728 | tf_op jit(solution)/shard_map/concatenate | solution.py:507
  13.0 7.9 %all-to-all-done.x0_ref.x_ref = bf16[16,144,128]{2,1,0:T(8,128)(2,1)S(1)} async-done(((bf16[16,144,128]{2,1,0:T(8,128)(2,1)}), bf16[16,144,128]{2,1,0:T(8,128)(2,1)S(1)}, u32[]{:S(2)}, u32[]{:S(2)}) %all-to-all-start) | async-done | bytes 589856 | tf_op jit(solution)/shard_map/all_to_all | solution.py:491
  20.8 1.9 %collective-permute-start = (bf16[16,144,128]{2,1,0:T(8,128)(2,1)S(1)}, bf16[16,144,128]{2,1,0:T(8,128)(2,1)S(1)}, u32[]{:S(2)}, u32[]{:S(2)}) collective-permute-start(bf16[16,144,128]{2,1,0:T(8,128)(2,1)S(1)} %all-to-all-done.x0_ref.x_ref), channel_id=1, source_target_pairs={{0,1},{1,0},{2,3},{3,2},{4,5},{5,4},{6,7},{7,6},{8,9},{9,8},{10,11... | collective-permute-start | bytes 1769480 | tf_op jit(solution)/shard_map/ppermute | solution.py:500
  22.7 4.0 %all-to-all-start.1 = ((bf16[32,192,128]{2,1,0:T(8,128)(2,1)}), bf16[32,192,128]{2,1,0:T(8,128)(2,1)S(1)}, u32[]{:S(2)}, u32[]{:S(2)}) async-start(bf16[32,192,128]{2,1,0:T(8,128)(2,1)} %pad_maximum_fusion), calls=%async_computation.1 | async-start | bytes 3145728 | tf_op jit(solution)/shard_map/all_to_all | solution.py:491
  26.6 0.0 collective-permute-done.x1_ref.x_ref
  26.7 17.0 %solve.1 = (f32[16,2,8,128]{3,2,1,0:T(8,128)}, f32[16,2,128,128]{3,2,1,0:T(8,128)}, bf16[16,2,256,128]{3,2,1,0:T(8,128)(2,1)}, bf16[16,2,256,128]{3,2,1,0:T(8,128)(2,1)}, bf16[16,2,128,256]{3,2,1,0:T(8,128)(2,1)}) custom-call(bf16[16,144,128]{2,1,0:T(8,128)(2,1)S(1)} %all-to-all-done.x0_ref.x_ref, bf16[16,144,128]{2,1,0:T(8,128)(2,1)S(1)} %collective-permute-done.x1_ref.x_ref), custom_call_target="tpu_custom_call" | custom-call | flops 16000000000 | bytes 20971520 | tf_op jit(solution)/shard_map/solve/pallas_call | solution.py:203
  43.7 5.6 %all-to-all-done.1 = bf16[32,192,128]{2,1,0:T(8,128)(2,1)S(1)} async-done(((bf16[32,192,128]{2,1,0:T(8,128)(2,1)}), bf16[32,192,128]{2,1,0:T(8,128)(2,1)S(1)}, u32[]{:S(2)}, u32[]{:S(2)}) %all-to-all-start.1) | async-done | bytes 1572896 | tf_op jit(solution)/shard_map/all_to_all | solution.py:491
  49.4 1.0 collective-permute-start.3
  50.3 0.0 copy-start
  50.3 0.0 copy-start.1
  50.3 5.3 %chain.1 = (bf16[4,4,2,256,256]{4,3,2,1,0:T(8,128)(2,1)S(1)}, f32[4,128,256]{2,1,0:T(8,128)S(1)}, f32[128,256]{1,0:T(8,128)S(1)}) custom-call(bf16[4,4,2,256,128]{4,3,2,1,0:T(8,128)(2,1)} %bitcast.31, bf16[4,4,2,128,256]{4,3,2,1,0:T(8,128)(2,1)} %bitcast.32, bf16[4,4,2,192,128]{4,3,2,1,0:T(8,128)(2,1)S(1)} %bitcast.17), custom_call_target="tpu_custom_call" | custom-call | flops 4000000000 | bytes 10485760 | tf_op jit(solution)/shard_map/chain/pallas_call | solution.py:269
  55.6 1.7 %collective-permute-start.1 = (f32[128,256]{1,0:T(8,128)S(1)}, f32[128,256]{1,0:T(8,128)S(1)}, u32[]{:S(2)}, u32[]{:S(2)}) collective-permute-start(f32[128,256]{1,0:T(8,128)S(1)} %get-tuple-element.36.own_ref), channel_id=1, source_target_pairs={{0,32},{8,40},{16,48},{24,56},{32,64},{40,72},{48,80},{56,88},{64,... | collective-permute-start | bytes 393224 | tf_op jit(solution)/shard_map/ppermute | solution.py:496
  57.4 0.0 copy-done
  57.4 0.0 copy-done.1
  57.4 0.0 copy-start.2
  57.4 2.4 %before_queries.1.e_ref = bf16[16,2,256,256]{3,2,1,0:T(8,128)(2,1)S(1)} custom-call(bf16[16,2,192,128]{3,2,1,0:T(8,128)(2,1)S(1)} %bitcast.18, f32[16,2,128,128]{3,2,1,0:T(8,128)S(1)} %copy-done, bf16[16,2,256,128]{3,2,1,0:T(8,128)(2,1)S(1)} %copy-done.1, bf16[16,2,256,256]{3,2,1,0:T(8,128)(2,1)S(1)} %bitcast.23), custom_call_target="tpu_custom_call" | custom-call | flops 4800000000 | bytes 8388608 | tf_op jit(solution)/shard_map/before_queries/pallas_call | solution.py:312
  59.8 5.4 %collective-permute-done.1.got_ref = f32[128,256]{1,0:T(8,128)S(1)} collective-permute-done((f32[128,256]{1,0:T(8,128)S(1)}, f32[128,256]{1,0:T(8,128)S(1)}, u32[]{:S(2)}, u32[]{:S(2)}) %collective-permute-start.1) | collective-permute-done | bytes 131104 | tf_op jit(solution)/shard_map/ppermute | solution.py:496
  65.1 0.2 shard_map.55
  65.3 0.1 collective-permute-start.2
  65.4 0.0 collective-permute-done.3
  65.4 0.0 copy-done.2
  65.5 4.0 %rows.2 = (bf16[16,128,256]{2,1,0:T(8,128)(2,1)S(1)}, f32[16,128,128]{2,1,0:T(8,128)S(1)}) custom-call(bf16[16,144,128]{2,1,0:T(8,128)(2,1)S(1)} %all-to-all-done.x0_ref.x_ref, bf16[16,2,192,128]{3,2,1,0:T(8,128)(2,1)S(1)} %bitcast.19, bf16[16,2,64,128]{3,2,1,0:T(8,128)(2,1)S(1)} %bitcast.21, f32[16,2,8,128]{3,2,1,0:T(8,128)S(1)} %copy-done.2, ...), custom_call_target="tpu_custom_call" | custom-call | flops 4800000000 | bytes 8388608 | tf_op jit(solution)/shard_map/rows/pallas_call | solution.py:360
  69.5 5.4 %collective-permute-done.2.got_ref = f32[128,256]{1,0:T(8,128)S(1)} collective-permute-done((f32[128,256]{1,0:T(8,128)S(1)}, f32[128,256]{1,0:T(8,128)S(1)}, u32[]{:S(2)}, u32[]{:S(2)}) %collective-permute-start.2) | collective-permute-done | bytes 131104 | tf_op jit(solution)/shard_map/ppermute | solution.py:496
  74.9 0.2 shard_map.56
  75.1 3.6 %collective-permute-start.4 = (f32[128,128]{1,0:T(8,128)S(1)}, f32[128,128]{1,0:T(8,128)S(1)}, u32[]{:S(2)}, u32[]{:S(2)}) collective-permute-start(f32[128,128]{1,0:T(8,128)S(1)} %get-tuple-element.51), channel_id=1, source_target_pairs={{0,128},{8,136},{16,144},{24,152},{32,160},{40,168},{48,176},{56,1... | collective-permute-start | bytes 196616 | tf_op jit(solution)/shard_map/ppermute | solution.py:496
  78.7 4.0 %rows.3 = (bf16[16,128,256]{2,1,0:T(8,128)(2,1)S(1)}, f32[16,128,128]{2,1,0:T(8,128)S(1)}) custom-call(bf16[16,144,128]{2,1,0:T(8,128)(2,1)S(1)} %collective-permute-done.x1_ref.x_ref, bf16[16,2,192,128]{3,2,1,0:T(8,128)(2,1)S(1)} %bitcast.20, bf16[16,2,64,128]{3,2,1,0:T(8,128)(2,1)S(1)} %bitcast.22, f32[16,2,8,128]{3,2,1,0:T(8,128)S(1)} %copy-done.2, ...), custom_call_target="tpu_custom_call" | custom-call | flops 4800000000 | bytes 8388608 | tf_op jit(solution)/shard_map/rows/pallas_call | solution.py:360
  82.7 0.0 collective-permute-done.4.got_ref
  82.7 2.2 %finish.1 = bf16[16,2,128,128]{3,2,1,0:T(8,128)(2,1)S(1)} custom-call(f32[128,128]{1,0:T(8,128)S(1)} %collective-permute-done.4.got_ref, f32[128,256]{1,0:T(8,128)S(1)} %get-tuple-element.52.longer_ref, f32[4,128,256]{2,1,0:T(8,128)S(1)} %get-tuple-element.53.start_ref, bf16[16,128,256]{2,1,0:T(8,128)(2,1)S(1)} %get-tuple-element.54.r0, ...), custom_call_target="tpu_custom_call" | custom-call | flops 1000000000 | bytes 5242880 | tf_op jit(solution)/shard_map/finish/pallas_call | solution.py:435
  85.0 22.4 %all_to_all.15 = bf16[32,128,128]{2,1,0:T(8,128)(2,1)S(1)} all-to-all(bf16[32,128,128]{2,1,0:T(8,128)(2,1)S(1)} %bitcast.16), channel_id=1, replica_groups={{0,1,2,3,4,5,6,7,8,9,10,11,12,13,14,15,16,17,18,19,20,21,22,23,24,25,26..., dimensions={0} | all-to-all | bytes 2097152 | tf_op jit(solution)/shard_map/all_to_all | solution.py:491
  107.3 1.6 %copy.18 = bf16[128,32,128]{2,1,0:T(8,128)(2,1)} copy(bf16[128,32,128]{2,0,1:T(8,128)(2,1)S(1)} %bitcast.27) | data formatting | bytes 2097152 | tf_op jit(solution)/shard_map/transpose | solution.py:523
  (1 shorter events, 0.0 us)
Async XLA Ops:
  0.0 11.5 %copy-start.3 = (bf16[128,16,128]{2,1,0:T(8,128)(2,1)S(1)}, bf16[128,16,128]{2,1,0:T(8,128)(2,1)}, u32[]{:S(2)}) copy-start(bf16[128,16,128]{2,1,0:T(8,128)(2,1)} %param.5) | copy-start | bytes 1572868
  2.2 18.6 %all-to-all-start = ((bf16[16,144,128]{2,1,0:T(8,128)(2,1)}), bf16[16,144,128]{2,1,0:T(8,128)(2,1)S(1)}, u32[]{:S(2)}, u32[]{:S(2)}) async-start(bf16[16,144,128]{2,1,0:T(8,128)(2,1)} %pack.1), calls=%async_computation | async-start | bytes 1179648 | tf_op jit(solution)/shard_map/all_to_all | solution.py:491
  20.8 5.8 %collective-permute-start = (bf16[16,144,128]{2,1,0:T(8,128)(2,1)S(1)}, bf16[16,144,128]{2,1,0:T(8,128)(2,1)S(1)}, u32[]{:S(2)}, u32[]{:S(2)}) collective-permute-start(bf16[16,144,128]{2,1,0:T(8,128)(2,1)S(1)} %all-to-all-done.x0_ref.x_ref), channel_id=1, source_target_pairs={{0,1},{1,0},{2,3},{3,2},{4,5},{5,4},{6,7},{7,6},{8,9},{9,8},{10,11... | collective-permute-start | bytes 1769480 | tf_op jit(solution)/shard_map/ppermute | solution.py:500
  22.7 26.6 %all-to-all-start.1 = ((bf16[32,192,128]{2,1,0:T(8,128)(2,1)}), bf16[32,192,128]{2,1,0:T(8,128)(2,1)S(1)}, u32[]{:S(2)}, u32[]{:S(2)}) async-start(bf16[32,192,128]{2,1,0:T(8,128)(2,1)} %pad_maximum_fusion), calls=%async_computation.1 | async-start | bytes 3145728 | tf_op jit(solution)/shard_map/all_to_all | solution.py:491
  49.4 16.1 %collective-permute-start.3 = (bf16[32,64,128]{2,1,0:T(8,128)(2,1)S(1)}, bf16[32,64,128]{2,1,0:T(8,128)(2,1)S(1)}, u32[]{:S(2)}, u32[]{:S(2)}) collective-permute-start(bf16[32,64,128]{2,1,0:T(8,128)(2,1)S(1)} %slice.4), channel_id=1, source_target_pairs={{0,1},{1,0},{2,3},{3,2},{4,5},{5,4},{6,7},{7,6},{8,9},{9,8},{10,11... | collective-permute-start | bytes 1572872 | tf_op jit(solution)/shard_map/ppermute | solution.py:500
  50.3 7.1 %copy-start = (f32[16,2,128,128]{3,2,1,0:T(8,128)S(1)}, f32[16,2,128,128]{3,2,1,0:T(8,128)}, u32[]{:S(2)}) copy-start(f32[16,2,128,128]{3,2,1,0:T(8,128)} %get-tuple-element.37.w_ref) | copy-start | bytes 6291460
  50.3 7.1 %copy-start.1 = (bf16[16,2,256,128]{3,2,1,0:T(8,128)(2,1)S(1)}, bf16[16,2,256,128]{3,2,1,0:T(8,128)(2,1)}, u32[]{:S(2)}) copy-start(bf16[16,2,256,128]{3,2,1,0:T(8,128)(2,1)} %get-tuple-element.38.tu_ref) | copy-start | bytes 6291460
  55.6 9.5 %collective-permute-start.1 = (f32[128,256]{1,0:T(8,128)S(1)}, f32[128,256]{1,0:T(8,128)S(1)}, u32[]{:S(2)}, u32[]{:S(2)}) collective-permute-start(f32[128,256]{1,0:T(8,128)S(1)} %get-tuple-element.36.own_ref), channel_id=1, source_target_pairs={{0,32},{8,40},{16,48},{24,56},{32,64},{40,72},{48,80},{56,88},{64,... | collective-permute-start | bytes 393224 | tf_op jit(solution)/shard_map/ppermute | solution.py:496
  57.4 8.1 %copy-start.2 = (f32[16,2,8,128]{3,2,1,0:T(8,128)S(1)}, f32[16,2,8,128]{3,2,1,0:T(8,128)}, u32[]{:S(2)}) copy-start(f32[16,2,8,128]{3,2,1,0:T(8,128)} %get-tuple-element.44.aux_ref) | copy-start | bytes 393220
  65.3 9.5 %collective-permute-start.2 = (f32[128,256]{1,0:T(8,128)S(1)}, f32[128,256]{1,0:T(8,128)S(1)}, u32[]{:S(2)}, u32[]{:S(2)}) collective-permute-start(f32[128,256]{1,0:T(8,128)S(1)} %get-tuple-element.42.run_ref), channel_id=1, source_target_pairs={{0,64},{8,72},{16,80},{24,88},{32,96},{40,104},{48,112},{56,120},{... | collective-permute-start | bytes 393224 | tf_op jit(solution)/shard_map/ppermute | solution.py:496
  75.1 7.6 %collective-permute-start.4 = (f32[128,128]{1,0:T(8,128)S(1)}, f32[128,128]{1,0:T(8,128)S(1)}, u32[]{:S(2)}, u32[]{:S(2)}) collective-permute-start(f32[128,128]{1,0:T(8,128)S(1)} %get-tuple-element.51), channel_id=1, source_target_pairs={{0,128},{8,136},{16,144},{24,152},{32,160},{40,168},{48,176},{56,1... | collective-permute-start | bytes 196616 | tf_op jit(solution)/shard_map/ppermute | solution.py:496
